TPU v7x, 512 devices: a whole 4x4x16 slice. The times are simulated.
512 devices in a mesh: row: 16 (over x, z_lo), col: 32 (over y, z_hi, core).
Axes of the slice: x: 4, y: 4, z: 16 (z_hi: 4, z_lo: 4; z = z_hi * 4 + z_lo), core: 2. Of those that a mesh axis runs over, the one named last changes fastest.
Arguments:
- out_grad: bfloat16 [1024, 8192], P('col', 'row'), may hold values from -6 to 6
- layer_input: bfloat16 [1024, 8192], P('col', 'row'), may hold values from -6 to 6
- gate_preact: bfloat16 [1024, 14784], P('row', 'col'), may hold values from -8 to 8
- up_preact: bfloat16 [1024, 14784], P('row', 'col'), may hold values from -6 to 6
- w_down: bfloat16 [8192, 14784], P('row', 'col'), may hold values from -0.0625 to 0.0625
- w_gate: bfloat16 [14784, 8192], P('col', 'row'), may hold values from -0.046875 to 0.046875
- w_up: bfloat16 [14784, 8192], P('col', 'row'), may hold values from -0.046875 to 0.046875
Outputs:
- input_grad: bfloat16 [1024, 8192], P('col', 'row')
- down_grad: bfloat16 [8192, 14784], P('row', 'col')
- gate_grad: bfloat16 [14784, 8192], P('col', 'row')
- up_grad: bfloat16 [14784, 8192], P('col', 'row')
All inputs are finite; a program needn't handle non-finite values.
Results may differ from a plain program's by a relative error of at most 0.005.
Values may be sent and summed in bfloat16 or wider, within the bound.
A program may use at most 64 MiB of HBM per device.

v0:
```python
import jax
import jax.numpy as jnp
from jax import lax
from jax.sharding import PartitionSpec as P


def silu_gated(gate_preact, up_preact):
    gate = gate_preact.astype(jnp.float32)
    return (gate * jax.nn.sigmoid(gate) * up_preact.astype(jnp.float32)).astype(jnp.bfloat16)


def swiglu_back(back_hidden, gate_preact, up_preact):
    gate = gate_preact.astype(jnp.float32)
    upper = up_preact.astype(jnp.float32)
    sig = jax.nn.sigmoid(gate)
    gate_back = (back_hidden * upper * sig * (1.0 + gate * (1.0 - sig))).astype(jnp.bfloat16)
    upward_back = (back_hidden * gate * sig).astype(jnp.bfloat16)
    return (gate_back, upward_back)


def contract_tokens(left, right):
    return lax.dot_general(
        left, right, (((0,), (0,)), ((), ())), preferred_element_type=jnp.float32
    )


def shards(out_grad, layer_input, gate_preact, up_preact, w_down, w_gate, w_up):
    grad_all, input_all = (
        lax.all_gather(out_grad, "col", axis=0, tiled=True),
        lax.all_gather(layer_input, "col", axis=0, tiled=True),
    )
    hidden = silu_gated(gate_preact, up_preact)
    hidden_all = lax.all_gather(hidden, "row", axis=0, tiled=True)
    back_hidden = lax.psum_scatter(
        jnp.dot(grad_all, w_down, preferred_element_type=jnp.float32),
        "row",
        scatter_dimension=0,
        tiled=True,
    )
    gate_back, upward_back = swiglu_back(back_hidden, gate_preact, up_preact)
    gate_all, upward_all = (
        lax.all_gather(gate_back, "row", axis=0, tiled=True),
        lax.all_gather(upward_back, "row", axis=0, tiled=True),
    )
    down_grad = contract_tokens(grad_all, hidden_all).astype(jnp.bfloat16)
    gate_grad = contract_tokens(gate_all, input_all).astype(jnp.bfloat16)
    up_grad = contract_tokens(upward_all, input_all).astype(jnp.bfloat16)
    first = jnp.dot(gate_all, w_gate, preferred_element_type=jnp.float32)
    input_sum = lax.psum_scatter(
        first + jnp.dot(upward_all, w_up, preferred_element_type=jnp.float32),
        "col",
        scatter_dimension=0,
        tiled=True,
    )
    input_grad = input_sum.astype(jnp.bfloat16)
    return (input_grad, down_grad, gate_grad, up_grad)


def solution(mesh):
    return jax.shard_map(
        shards,
        mesh=mesh,
        in_specs=(
            P("col", "row"),
            P("col", "row"),
            P("row", "col"),
            P("row", "col"),
            P("row", "col"),
            P("col", "row"),
            P("col", "row"),
        ),
        out_specs=(P("col", "row"), P("row", "col"), P("col", "row"), P("col", "row")),
        check_vma=False,
    )
```

profile of v0, /device:TPU:24, one launch (start us, length us, event | category | flops | bytes accessed | tf_op | source)
XLA Modules:
  0.0 414.3 jit_solution(10404487065694558398)
XLA Ops:
  7.2 0.0 copy-start
  7.2 0.0 all-gather.3.cloned.1.call-start
  7.2 0.7 all-gather.3.cloned.1.call-update
  7.9 0.0 copy-start.3
  7.9 0.0 copy-start.4
  7.9 0.0 reduce-scatter.3.cloned.1.call-start
  8.0 77.2 %all-gather.3.cloned.1.call-done = bf16[1024,512]{1,0:T(8,128)(2,1)} async-done(((bf16[32,512]{1,0:T(8,128)(2,1)}), bf16[1024,512]{1,0:T(8,128)(2,1)}) %all-gather.3.cloned.1.call-update) | async-done | bytes 1048592 | tf_op jit(solution)/shard_map/all_gather | solution.py:29
  85.1 3.4 fusion.11
  88.5 0.0 reduce-scatter.3.cloned.1.call-update
  88.6 0.0 all-gather.5.cloned.1.call-start
  88.6 0.7 all-gather.5.cloned.1.call-update
  89.3 0.0 reduce-scatter.5.cloned.1.call-start
  89.4 92.7 %reduce-scatter.3.cloned.1.call-done = f32[64,462]{1,0:T(8,128)} async-done(((f32[1024,462]{1,0:T(8,128)}), f32[64,462]{1,0:T(8,128)}) %reduce-scatter.3.cloned.1.call-update) | async-done | bytes 118288 | tf_op jit(solution)/shard_map/reduce_scatter | solution.py:34
  182.1 0.0 copy-done.3
  182.1 0.0 copy-done.4
  182.1 1.0 fusion.10
  183.1 48.0 %all_gather.16 = bf16[1024,462]{1,0:T(8,128)(2,1)S(1)} all-gather(bf16[64,462]{1,0:T(8,128)(2,1)S(1)} %get-tuple-element.5), channel_id=1, replica_groups=mesh['row'=16,'col'=32] {'row'}, dimensions={0}, use_global_device_ids=true | all-gather | bytes 1005312 | tf_op jit(solution)/shard_map/all_gather | solution.py:42
  231.0 0.0 copy-done
  231.0 0.7 fusion.12
  231.7 50.9 %all_gather.17 = bf16[1024,462]{1,0:T(8,128)(2,1)S(1)} all-gather(bf16[64,462]{1,0:T(8,128)(2,1)S(1)} %get-tuple-element.4), channel_id=1, replica_groups=mesh['row'=16,'col'=32] {'row'}, dimensions={0}, use_global_device_ids=true | all-gather | bytes 1005312 | tf_op jit(solution)/shard_map/all_gather | solution.py:43
  282.6 0.0 copy-done.2
  282.6 2.0 convolution_add_fusion
  284.6 0.0 reduce-scatter.5.cloned.1.call-update
  284.7 0.0 all-gather.5.cloned.1.call-done
  284.7 0.0 copy-start.5
  284.7 2.8 convolution_convert_fusion
  287.5 1.5 convolution_convert_fusion.1
  288.9 46.3 %all_gather.18 = bf16[1024,462]{1,0:T(8,128)(2,1)S(1)} all-gather(bf16[64,462]{1,0:T(8,128)(2,1)S(1)} %get-tuple-element.6), channel_id=1, replica_groups=mesh['row'=16,'col'=32] {'row'}, dimensions={0}, use_global_device_ids=true | all-gather | bytes 1005312 | tf_op jit(solution)/shard_map/all_gather | solution.py:33
  335.3 0.0 copy-done.1
  335.3 1.5 fusion
  336.7 69.5 %reduce-scatter.5.cloned.1.call-done = f32[32,512]{1,0:T(8,128)} async-done(((f32[1024,512]{1,0:T(8,128)}), f32[32,512]{1,0:T(8,128)}) %reduce-scatter.5.cloned.1.call-update) | async-done | bytes 65552 | tf_op jit(solution)/shard_map/reduce_scatter | solution.py:49
  406.3 1.5 convert_element_type.36
  (3 shorter events, 0.0 us)
Async XLA Ops:
  7.2 223.9 %copy-start = (bf16[462,512]{1,0:T(8,128)(2,1)S(1)}, bf16[462,512]{1,0:T(8,128)(2,1)}, u32[]{:S(2)}) copy-start(bf16[462,512]{1,0:T(8,128)(2,1)} %param.12) | copy-start | bytes 1419268
  7.2 78.0 %all-gather.3.cloned.1.call-start = ((), (), s32[]{:S(2)}) async-start(), calls=%async_computation.2 | async-start | bytes 1081344 | tf_op jit(solution)/shard_map/all_gather | solution.py:29
  7.9 174.2 %copy-start.3 = (bf16[64,462]{1,0:T(8,128)(2,1)S(1)}, bf16[64,462]{1,0:T(8,128)(2,1)}, u32[]{:S(2)}) copy-start(bf16[64,462]{1,0:T(8,128)(2,1)} %param.9) | copy-start | bytes 177412
  7.9 174.1 %copy-start.4 = (bf16[64,462]{1,0:T(8,128)(2,1)S(1)}, bf16[64,462]{1,0:T(8,128)(2,1)}, u32[]{:S(2)}) copy-start(bf16[64,462]{1,0:T(8,128)(2,1)} %param.10) | copy-start | bytes 177412
  7.9 174.1 %reduce-scatter.3.cloned.1.call-start = ((), (), s32[]{:S(2)}) async-start(), calls=%async_computation.3 | async-start | bytes 2228224 | tf_op jit(solution)/shard_map/reduce_scatter | solution.py:34
  88.6 196.1 %all-gather.5.cloned.1.call-start = ((), (), s32[]{:S(2)}) async-start(), calls=%async_computation.5 | async-start | bytes 1081344 | tf_op jit(solution)/shard_map/all_gather | solution.py:30
  89.3 317.0 %reduce-scatter.5.cloned.1.call-start = ((), (), s32[]{:S(2)}) async-start(), calls=%async_computation.4 | async-start | bytes 2162688 | tf_op jit(solution)/shard_map/reduce_scatter | solution.py:49
  231.0 51.6 %copy-start.2 = (bf16[462,512]{1,0:T(8,128)(2,1)S(1)}, bf16[462,512]{1,0:T(8,128)(2,1)}, u32[]{:S(2)}) copy-start(bf16[462,512]{1,0:T(8,128)(2,1)} %param.13) | copy-start | bytes 1419268
  284.7 2.8 copy-start.5
  287.5 47.8 %copy-start.1 = (bf16[1024,512]{1,0:T(8,128)(2,1)S(1)}, bf16[1024,512]{1,0:T(8,128)(2,1)}, u32[]{:S(2)}) copy-start(bf16[1024,512]{1,0:T(8,128)(2,1)} %all-gather.3.cloned.1.call-done) | copy-start | bytes 3145732
Sparse Core Ops, SparseCore 0:
  11.2 73.9 all-gather.2
  88.7 93.3 reduce-scatter.2
  185.2 67.4 all-gather.4
  284.8 121.4 reduce-scatter.4
where the time goes:
time: 416 us; the launch traced here: 414 us
  waiting for transfers between devices  241 us (58%)
  blocking collectives  145 us (35%)
  between operations  13.8 us (3%)
  matrix products  11.8 us (3%)
    reduce_scatter x1, waiting for transfers between devices, shards(): lax.psum_scatter(jnp.dot(grad_all, w_down, preferred_element_type=jnp.flo...  92.7 us
    all_gather x1, waiting for transfers between devices, shards(): lax.all_gather(out_grad, 'col', axis=0, tiled=True)  77.2 us
    reduce_scatter x1, waiting for transfers between devices, shards(): lax.psum_scatter(first + jnp.dot(upward_all, w_up, preferred_element_type...  69.5 us
    all_gather x1, blocking collectives, shards(): lax.all_gather(upward_back, 'row', axis=0, tiled=True)  50.9 us
    all_gather x1, blocking collectives, shards(): lax.all_gather(gate_back, 'row', axis=0, tiled=True)  48 us
    all_gather x1, blocking collectives, shards(): hidden_all = lax.all_gather(hidden, 'row', axis=0, tiled=True)  46.3 us
  transfers between devices with their start and end apart: 4, of which 3 were waited for; matrix products, arithmetic and copies ran while one was open for 2% of the time, Pallas kernels for 0%

commit v1 on v0

v1 whole, which is shorter than its diff:
```python
import functools

import jax
import jax.numpy as jnp
from jax import lax
from jax.experimental import pallas as pl
from jax.experimental.pallas import tpu as pltpu
from jax.sharding import PartitionSpec as P

BF = jnp.bfloat16
F32 = jnp.float32
MESH = pl.DeviceIdType.MESH
N_COPIES = 128
WIDE = 512


def rounded(value):
    return value.astype(BF)


def dot(left, right, dims):
    return lax.dot_general(left, right, (dims, ((), ())), preferred_element_type=F32)


NN = ((1,), (0,))
NT = ((1,), (1,))
TN = ((0,), (0,))


def kernel(
    og_in, li_in, gp_in, up_in, wd_in, wg_in, wu_in,
    ig_out, dg_out, gg_out, ug_out,
    grads, inputs, hidden, backs,
    gp, up, wd_raw, wg_raw, wu_raw, wd, wg, wu,
    part, part_bf, far_lo, far_hi, from_lo, from_hi, z_send, z_recv,
    ipart, ipart_sib, iq, iq_bf, ifar_lo, ifar_hi, ifrom_lo, ifrom_hi, iz_send, iz_recv,
    gg_acc, ug_acc, gg, ug, dg, ig,
    local_sem, send_sem, recv_sem,
):
    units = gp_in.shape[1]
    row, col = lax.axis_index("row"), lax.axis_index("col")
    x, zl = lax.div(row, 4), lax.rem(row, 4)
    y, zh, core = lax.div(col, 8), lax.rem(lax.div(col, 2), 4), lax.rem(col, 2)
    sib = 1 - core

    def on(value, step):
        return lax.rem(value + step + 4, 4)

    xp, xm, xo = on(x, 1), on(x, -1), on(x, 2)
    yp, ym, yo = on(y, 1), on(y, -1), on(y, 2)
    hp, hm, ho = on(zh, 1), on(zh, -1), on(zh, 2)

    def row_of(a, b):
        return a * 4 + b

    def col_of(a, b, k):
        return (a * 4 + b) * 2 + k

    X_UP, X_DN = (row_of(xp, zl), col), (row_of(xm, zl), col)
    Y_UP, Y_DN = (row, col_of(yp, zh, core)), (row, col_of(ym, zh, core))
    H_UP, H_DN, H_OP = (
        (row, col_of(y, hp, core)),
        (row, col_of(y, hm, core)),
        (row, col_of(y, ho, core)),
    )
    L_TO = [(row_of(x, on(zl, d)), col) for d in (1, 2, 3)]
    SIB = (row, col_of(y, zh, sib))

    locals_ = []

    def local(src, dst):
        copy = pltpu.make_async_copy(src, dst, local_sem.at[len(locals_)])
        locals_.append(copy)
        copy.start()
        return copy

    sent = []

    def send(src, dst, where):
        k = len(sent)
        copy = pltpu.make_async_remote_copy(
            src_ref=src,
            dst_ref=dst,
            send_sem=send_sem.at[k],
            recv_sem=recv_sem.at[k],
            device_id=where,
            device_id_type=MESH,
        )
        copy.start()
        sent.append(copy)
        return copy

    own = row_of(y, zh)
    c_og = local(og_in, grads.at[own, core])
    c_gp = local(gp_in, gp)
    c_up = local(up_in, up)
    c_wd = local(wd_in, wd_raw)
    c_li = local(li_in, inputs.at[own, core])
    c_wg = local(wg_in, wg_raw)
    c_wu = local(wu_in, wu_raw)

    barrier = pltpu.get_barrier_semaphore()
    partners = [X_UP, X_DN, Y_UP, Y_DN, H_UP, H_DN, H_OP, SIB] + L_TO
    for where in partners:
        pl.semaphore_signal(barrier, inc=1, device_id=where, device_id_type=MESH)
    pl.semaphore_wait(barrier, len(partners))

    def share(block):
        ref = grads.at[row_of(y, block), core]
        return send(ref, ref, Y_UP), send(ref, ref, Y_DN), send(ref, ref, SIB)

    def here(ref, index):
        return ref.at[index, core]

    g_up = send(og_in, here(grads, own), H_UP)
    g_dn = send(og_in, here(grads, own), H_DN)
    y0 = (
        send(og_in, here(grads, own), Y_UP),
        send(og_in, here(grads, own), Y_DN),
        send(og_in, here(grads, own), SIB),
    )

    c_gp.wait()
    c_up.wait()
    gate = gp[...].astype(F32)
    upper = up[...].astype(F32)
    sig = jax.nn.sigmoid(gate)
    hidden[row] = jnp.zeros((64, WIDE), BF)
    hidden[row, :, 0:units] = rounded(gate * sig * upper)
    c_wd.wait()
    wd[...] = jnp.zeros((WIDE, wd.shape[1]), BF)
    wd[0:units, :] = wd_raw[...]

    y0[0].wait_recv()
    ref = here(grads, row_of(ym, zh))
    f_up0 = send(ref, ref, Y_UP)
    g_up.wait_recv()
    ref = grads.at[row_of(y, hm), core, pl.ds(0, 16)]
    g_up2 = send(ref, ref, H_UP)
    y1 = share(hm)
    g_dn.wait_recv()
    ref = grads.at[row_of(y, hp), core, pl.ds(16, 16)]
    g_dn2 = send(ref, ref, H_DN)
    y2 = share(hp)
    y1[1].wait_recv()
    ref = here(grads, row_of(yp, hm))
    f_dn1 = send(ref, ref, Y_DN)
    y2[0].wait_recv()
    ref = here(grads, row_of(ym, hp))
    f_up2 = send(ref, ref, Y_UP)
    g_up2.wait_recv()
    g_dn2.wait_recv()
    y3 = share(ho)

    i_up = send(li_in, here(inputs, own), H_UP)
    i_dn = send(li_in, here(inputs, own), H_DN)
    h_z = [send(hidden.at[row], hidden.at[row], where) for where in L_TO]

    def plane(ref, a):
        return ref.at[pl.ds(a * 4, 4)]

    def plane_core(ref, a, k):
        return ref.at[pl.ds(a * 4, 4), k]

    def partial(a):
        rows = grads[pl.ds(a * 4, 4)].reshape(256, grads.shape[3])
        out = dot(rows, wd[...], NT).reshape(4, 64, WIDE)
        part[pl.ds(a * 4, 4)] = out
        part_bf[pl.ds(a * 4, 4)] = rounded(out)

    y3[1].wait_recv()
    ref = here(grads, row_of(yp, ho))
    f_dn3 = send(ref, ref, Y_DN)
    c_og.wait()
    y0[2].wait_recv()
    y1[2].wait_recv()
    y2[2].wait_recv()
    y3[2].wait_recv()
    partial(y)
    y1[0].wait_recv()
    y3[0].wait_recv()
    s_ym = send(plane_core(grads, ym, core), plane_core(grads, ym, core), SIB)
    y0[1].wait_recv()
    y2[1].wait_recv()
    s_yp = send(plane_core(grads, yp, core), plane_core(grads, yp, core), SIB)
    s_ym.wait_recv()
    partial(ym)
    f_up0.wait_recv()
    f_up2.wait_recv()
    f_dn1.wait_recv()
    f_dn3.wait_recv()
    s_yo = send(plane_core(grads, yo, core), plane_core(grads, yo, core), SIB)
    s_yp.wait_recv()
    partial(yp)
    s_yo.wait_recv()
    partial(yo)

    def two(ref, a, b):
        return ref.at[pl.ds(a * 4 + b, 2)]

    r_up = send(two(part_bf, xo, 0), far_lo, X_UP)
    r_dn = send(two(part_bf, xo, 2), far_hi, X_DN)
    e_up = send(two(part_bf, xp, 2), from_lo.at[pl.ds(2, 2)], X_UP)
    e_dn = send(two(part_bf, xm, 0), from_hi.at[pl.ds(0, 2)], X_DN)

    i_up.wait_recv()
    ref = inputs.at[row_of(y, hm), core, pl.ds(0, 16)]
    i_up2 = send(ref, ref, H_UP)
    i_dn.wait_recv()
    ref = inputs.at[row_of(y, hp), core, pl.ds(16, 16)]
    i_dn2 = send(ref, ref, H_DN)

    r_up.wait_recv()
    part_bf[pl.ds(xp * 4, 2)] = rounded(part[pl.ds(xp * 4, 2)] + far_lo[...].astype(F32))
    l_up = send(two(part_bf, xp, 0), from_lo.at[pl.ds(0, 2)], X_UP)
    r_dn.wait_recv()
    part_bf[pl.ds(xm * 4 + 2, 2)] = rounded(part[pl.ds(xm * 4 + 2, 2)] + far_hi[...].astype(F32))
    l_dn = send(two(part_bf, xm, 2), from_hi.at[pl.ds(2, 2)], X_DN)

    i_up2.wait_recv()
    i_dn2.wait_recv()
    c_li.wait()
    ref = plane_core(inputs, y, core)
    iy_up, iy_dn, iy_s = send(ref, ref, Y_UP), send(ref, ref, Y_DN), send(ref, ref, SIB)

    def hidden_x(b):
        ref = hidden.at[row_of(x, b)]
        return send(ref, ref, X_UP), send(ref, ref, X_DN)

    hx = [hidden_x(zl)]
    for d in (1, 2, 3):
        h_z[d - 1].wait_recv()
        hx.append(hidden_x(on(zl, -d)))

    c_wg.wait()
    c_wu.wait()
    wg[...] = jnp.zeros((WIDE, wg.shape[1]), BF)
    wg[0:units, :] = wg_raw[...]
    wu[...] = jnp.zeros((WIDE, wu.shape[1]), BF)
    wu[0:units, :] = wu_raw[...]

    e_up.wait_recv()
    e_dn.wait_recv()
    l_up.wait_recv()
    l_dn.wait_recv()

    def x_sum(b):
        return part[row_of(x, b)] + from_lo[b].astype(F32) + from_hi[b].astype(F32)

    t_z = []
    for d in (1, 2, 3):
        z_send[d - 1] = rounded(x_sum(on(zl, d)))
        t_z.append(send(z_send.at[d - 1], z_recv.at[d - 1], L_TO[d - 1]))
    back = x_sum(zl)

    iy_up.wait_recv()
    ref = inputs.at[pl.ds(ym * 4, 2), core]
    if_up = send(ref, ref, Y_UP)
    iy_dn.wait_recv()
    ref = inputs.at[pl.ds(yp * 4 + 2, 2), core]
    if_dn = send(ref, ref, Y_DN)
    is_m = send(plane_core(inputs, ym, core), plane_core(inputs, ym, core), SIB)
    is_p = send(plane_core(inputs, yp, core), plane_core(inputs, yp, core), SIB)

    for d in (1, 2, 3):
        t_z[d - 1].wait_recv()
        back = back + z_recv[d - 1].astype(F32)
    back = back[:, 0:units]
    backs[row] = jnp.zeros((2, 64, WIDE), BF)
    backs[row, 0, :, 0:units] = rounded(back * upper * sig * (1.0 + gate * (1.0 - sig)))
    backs[row, 1, :, 0:units] = rounded(back * gate * sig)

    ref = backs.at[row]
    b_z = [send(ref, ref, where) for where in L_TO]

    def backs_x(b):
        ref = backs.at[row_of(x, b)]
        return send(ref, ref, X_UP), send(ref, ref, X_DN)

    bx = [backs_x(zl)]

    if_up.wait_recv()
    if_dn.wait_recv()
    is_o = send(plane_core(inputs, yo, core), plane_core(inputs, yo, core), SIB)

    def forward(ref, a, b, where):
        block = ref.at[row_of(a, b)]
        return send(block, block, where)

    bf = []
    for d in (1, 2, 3):
        b_z[d - 1].wait_recv()
        bx.append(backs_x(on(zl, -d)))
        if d == 1:
            bx[0][0].wait_recv()
            bf.append(forward(backs, xm, zl, X_UP))
        if d == 2:
            bx[1][1].wait_recv()
            bf.append(forward(backs, xp, on(zl, -1), X_DN))

    iy_s.wait_recv()
    is_m.wait_recv()
    is_p.wait_recv()
    is_o.wait_recv()

    sib_copies = []

    def use(a, first):
        gate_rows = backs[pl.ds(a * 4, 4), 0].reshape(256, WIDE)
        up_rows = backs[pl.ds(a * 4, 4), 1].reshape(256, WIDE)
        out = dot(gate_rows, wg[...], NN) + dot(up_rows, wu[...], NN)
        ipart[pl.ds(a * 4, 4)] = out.reshape(4, 2, 32, out.shape[1])
        sib_copies.append(send(plane_core(ipart, a, sib), plane(ipart_sib, a), SIB))
        in_rows = inputs[pl.ds(a * 4, 4)].reshape(256, inputs.shape[3])
        gate_sum, up_sum = dot(gate_rows, in_rows, TN), dot(up_rows, in_rows, TN)
        if first:
            gg_acc[...] = gate_sum
            ug_acc[...] = up_sum
        else:
            gg_acc[...] += gate_sum
            ug_acc[...] += up_sum

    use(x, True)
    bx[2][0].wait_recv()
    bf.append(forward(backs, xm, on(zl, -2), X_UP))
    bx[3][1].wait_recv()
    bf.append(forward(backs, xp, on(zl, -3), X_DN))
    bx[1][0].wait_recv()
    bx[3][0].wait_recv()
    use(xm, False)
    bx[0][1].wait_recv()
    bx[2][1].wait_recv()
    use(xp, False)
    for k in range(4):
        hx[k][0].wait_recv()
        hx[k][1].wait_recv()
    hf = [
        forward(hidden, xm, zl, X_UP),
        forward(hidden, xm, on(zl, -1), X_UP),
        forward(hidden, xp, on(zl, -2), X_DN),
        forward(hidden, xp, on(zl, -3), X_DN),
    ]
    for copy in bf:
        copy.wait_recv()
    use(xo, False)

    for copy in sib_copies:
        copy.wait_recv()
    for a in range(4):
        out = ipart[pl.ds(a * 4, 4), core] + ipart_sib[pl.ds(a * 4, 4)]
        iq[pl.ds(a * 4, 4)] = out
        iq_bf[pl.ds(a * 4, 4)] = rounded(out)

    q_up = send(two(iq_bf, yo, 0), ifar_lo, Y_UP)
    q_dn = send(two(iq_bf, yo, 2), ifar_hi, Y_DN)
    qe_up = send(two(iq_bf, yp, 2), ifrom_lo.at[pl.ds(2, 2)], Y_UP)
    qe_dn = send(two(iq_bf, ym, 0), ifrom_hi.at[pl.ds(0, 2)], Y_DN)

    gg[...] = rounded(gg_acc[0:units, :])
    ug[...] = rounded(ug_acc[0:units, :])
    c_gg = local(gg, gg_out)
    c_ug = local(ug, ug_out)

    q_up.wait_recv()
    iq_bf[pl.ds(yp * 4, 2)] = rounded(iq[pl.ds(yp * 4, 2)] + ifar_lo[...].astype(F32))
    ql_up = send(two(iq_bf, yp, 0), ifrom_lo.at[pl.ds(0, 2)], Y_UP)
    q_dn.wait_recv()
    iq_bf[pl.ds(ym * 4 + 2, 2)] = rounded(iq[pl.ds(ym * 4 + 2, 2)] + ifar_hi[...].astype(F32))
    ql_dn = send(two(iq_bf, ym, 2), ifrom_hi.at[pl.ds(2, 2)], Y_DN)

    for copy in hf:
        copy.wait_recv()
    h_rows = hidden[...].reshape(1024, WIDE)
    g_rows = grads[...].reshape(1024, grads.shape[3])
    dg[...] = rounded(dot(h_rows, g_rows, TN)[0:units, :])
    c_dg = local(dg, dg_out)

    qe_up.wait_recv()
    qe_dn.wait_recv()
    ql_up.wait_recv()
    ql_dn.wait_recv()

    def y_sum(b):
        return iq[row_of(y, b)] + ifrom_lo[b].astype(F32) + ifrom_hi[b].astype(F32)

    t_h = []
    for d, where in ((1, H_UP), (2, H_OP), (3, H_DN)):
        iz_send[d - 1] = rounded(y_sum(on(zh, d)))
        t_h.append(send(iz_send.at[d - 1], iz_recv.at[d - 1], where))
    total = y_sum(zh)
    for d in (1, 2, 3):
        t_h[d - 1].wait_recv()
        total = total + iz_recv[d - 1].astype(F32)
    ig[...] = rounded(total)
    c_ig = local(ig, ig_out)

    for copy in sent:
        copy.wait_send()
    for copy in (c_gg, c_ug, c_dg, c_ig):
        copy.wait()


def shards(out_grad, layer_input, gate_preact, up_preact, w_down, w_gate, w_up):
    tokens, feats = out_grad.shape
    units = gate_preact.shape[1]
    vm = pltpu.VMEM
    whole = (16, 2, 32, feats)
    ig, dg, gg, ug = pl.pallas_call(
        kernel,
        out_shape=(
            jax.ShapeDtypeStruct((tokens, feats), BF),
            jax.ShapeDtypeStruct((units, feats), BF),
            jax.ShapeDtypeStruct((units, feats), BF),
            jax.ShapeDtypeStruct((units, feats), BF),
        ),
        in_specs=[pl.BlockSpec(memory_space=pl.ANY)] * 7,
        out_specs=(pl.BlockSpec(memory_space=pl.ANY),) * 4,
        scratch_shapes=[
            vm(whole, BF), vm(whole, BF), vm((16, 64, WIDE), BF), vm((16, 2, 64, WIDE), BF),
            vm((64, units), BF), vm((64, units), BF),
            vm((units, feats), BF), vm((units, feats), BF), vm((units, feats), BF),
            vm((WIDE, feats), BF), vm((WIDE, feats), BF), vm((WIDE, feats), BF),
            vm((16, 64, WIDE), F32), vm((16, 64, WIDE), BF),
            vm((2, 64, WIDE), BF), vm((2, 64, WIDE), BF),
            vm((4, 64, WIDE), BF), vm((4, 64, WIDE), BF),
            vm((3, 64, WIDE), BF), vm((3, 64, WIDE), BF),
            vm(whole, F32), vm((16, 32, feats), F32),
            vm((16, 32, feats), F32), vm((16, 32, feats), BF),
            vm((2, 32, feats), BF), vm((2, 32, feats), BF),
            vm((4, 32, feats), BF), vm((4, 32, feats), BF),
            vm((3, 32, feats), BF), vm((3, 32, feats), BF),
            vm((WIDE, feats), F32), vm((WIDE, feats), F32),
            vm((units, feats), BF), vm((units, feats), BF), vm((units, feats), BF),
            vm((tokens, feats), BF),
            pltpu.SemaphoreType.DMA((16,)),
            pltpu.SemaphoreType.DMA((N_COPIES,)),
            pltpu.SemaphoreType.DMA((N_COPIES,)),
        ],
        compiler_params=pltpu.CompilerParams(
            collective_id=0, has_side_effects=True, vmem_limit_bytes=48 * 1024 * 1024
        ),
        cost_estimate=pl.CostEstimate(
            flops=12 * 1024 * units * feats, bytes_accessed=3_000_000, transcendentals=64 * units
        ),
        name="swiglu_back",
    )(out_grad, layer_input, gate_preact, up_preact, w_down.T, w_gate, w_up)
    return ig, dg.T, gg, ug


def solution(mesh):
    return jax.shard_map(
        shards,
        mesh=mesh,
        in_specs=(
            P("col", "row"),
            P("col", "row"),
            P("row", "col"),
            P("row", "col"),
            P("row", "col"),
            P("col", "row"),
            P("col", "row"),
        ),
        out_specs=(P("col", "row"), P("row", "col"), P("col", "row"), P("col", "row")),
        check_vma=False,
    )
```

time: 416 us -> 112 us (0.27)
  waiting for transfers between devices: 241 us -> 0 us
  blocking collectives: 145 us -> 0 us
  Pallas kernels: 0 us -> 101 us
  between operations: 13.8 us -> 0.66 us
  matrix products: 11.8 us -> 0 us
  local copies, waits for them, and re-layouts: 0.03 us -> 9.19 us
    reduce_scatter x2 -> x0, waiting for transfers between devices: 162 us -> none  [the longest x1 92.7 us: shards(): lax.psum_scatter(jnp.dot(grad_all, w_down, preferred_element_type=jnp.flo...]
    all_gather x3 -> x0, blocking collectives: 145 us -> none  [the longest x1 50.9 us: shards(): lax.all_gather(upward_back, 'row', axis=0, tiled=True)]
    pallas_call x0 -> x1, Pallas kernels: none -> 101 us  [shards(): pl.pallas_call(kernel, out_shape=(jax.ShapeDtypeStruct((tokens, feats), B...]
    all_gather x2 -> x0, waiting for transfers between devices: 77.2 us -> none  [the longest x1 77.2 us: shards(): lax.all_gather(out_grad, 'col', axis=0, tiled=True)]
    dot_general x6 -> x0, matrix products: 11.8 us -> none  [the longest x3 5.7 us: contract_tokens(): lax.dot_general(left, right, (((0,), (0,)), ((), ())), preferred_element_...]
    unnamed x12 -> x18, local copies, waits for them, and re-layouts: 0.03 us -> 9.19 us
  transfers between devices with their start and end apart: 4 -> 0, of which waited for: 3 -> 0; matrix products, arithmetic and copies ran while one was open for 2% -> 0% of each run, Pallas kernels for 0% -> 0%
where the time goes in v1:
time: 112 us; the launch traced here: 111 us
  Pallas kernels  101 us (90%)
  local copies, waits for them, and re-layouts  9.19 us (8%)
    pallas_call x1, Pallas kernels, shards(): pl.pallas_call(kernel, out_shape=(jax.ShapeDtypeStruct((tokens, feats), B...  101 us
    unnamed x18, local copies, waits for them, and re-layouts  9.19 us

profile of v1, /device:TPU:24, one launch (start us, length us, event | category | flops | bytes accessed | tf_op | source)
XLA Modules:
  0.0 110.7 jit_solution(1263105783128328471)
XLA Ops:
  0.6 0.0 copy-start
  0.6 1.0 copy-done
  1.7 0.0 copy-start.1
  1.7 1.0 copy-done.1
  2.7 0.0 copy-start.2
  2.7 1.0 copy-done.2
  3.7 0.0 copy-start.3
  3.7 0.8 copy-done.3
  4.5 0.0 copy-start.4
  4.5 0.8 copy-done.4
  5.4 0.0 copy-start.5
  5.4 0.8 copy-done.5
  6.1 0.0 copy-start.6
  6.1 0.8 copy-done.6
  6.9 100.8 %swiglu_back.1 = (bf16[32,512]{1,0:T(8,128)(2,1)S(1)}, bf16[462,512]{1,0:T(8,128)(2,1)S(1)}, bf16[462,512]{1,0:T(8,128)(2,1)S(1)}, bf16[462,512]{1,0:T(8,128)(2,1)S(1)}) custom-call(bf16[32,512]{1,0:T(8,128)(2,1)S(1)} %copy-done.5, bf16[32,512]{1,0:T(8,128)(2,1)S(1)} %copy-done.6, bf16[64,462]{1,0:T(8,128)(2,1)S(1)} %copy-done.3, ...), custom_call_target="tpu_custom_call" | custom-call | flops 2906652672 | bytes 3000000 | tf_op jit(solution)/shard_map/swiglu_back/pallas_call | solution.py:408
  107.7 0.6 copy.15
  108.3 0.8 copy.16
  109.1 0.8 copy.17
  109.9 0.8 copy.18
Async XLA Ops:
  0.6 1.0 copy-start
  1.7 1.0 copy-start.1
  2.7 1.0 copy-start.2
  3.7 0.8 copy-start.3
  4.5 0.8 copy-start.4
  5.4 0.8 copy-start.5
  6.1 0.8 copy-start.6

commit v2 on v0

v2 whole, which is shorter than its diff:
```python
import jax
import jax.numpy as jnp
from jax import lax
from jax.experimental import pallas as pl
from jax.experimental.pallas import tpu as pltpu
from jax.sharding import PartitionSpec as P

BF = jnp.bfloat16
F32 = jnp.float32
MESH = pl.DeviceIdType.MESH
N_COPIES = 128
WIDE = 512
PARTS = 2
RT = 32 // PARTS
VMEM_ALL = 64 * 1024 * 1024 - 65536


def rounded(value):
    return value.astype(BF)


def dot(left, right, dims):
    return lax.dot_general(left, right, (dims, ((), ())), preferred_element_type=F32)


NN = ((1,), (0,))
NT = ((1,), (1,))
TN = ((0,), (0,))


def kernel(
    og_in, li_in, gp_in, up_in, wd_in, wg_in, wu_in,
    ig_out, dg_out, gg_out, ug_out,
    grads, inputs, hidden, backs, backs_sib,
    gp, up, pre, wd_raw, wg_raw, wu_raw, wd, wg, wu,
    part, part_bf, far_lo, far_hi, from_lo, from_hi, z_send, z_recv,
    iq, iq_bf, i_recv, iz_send, iz_recv,
    gg, ug, dg, ig,
    local_sem, send_sem, recv_sem,
):
    units = gp_in.shape[1]
    feats = og_in.shape[2]
    row, col = lax.axis_index("row"), lax.axis_index("col")
    x, zl = lax.div(row, 4), lax.rem(row, 4)
    y, zh, core = lax.div(col, 8), lax.rem(lax.div(col, 2), 4), lax.rem(col, 2)
    sib = 1 - core

    def on(value, step):
        return lax.rem(value + step + 4, 4)

    xp, xm, xo = on(x, 1), on(x, -1), on(x, 2)
    yp, ym, yo = on(y, 1), on(y, -1), on(y, 2)
    hp, hm, ho = on(zh, 1), on(zh, -1), on(zh, 2)

    def at(a, b):
        return a * 4 + b

    X_UP, X_DN = (at(xp, zl), col), (at(xm, zl), col)
    Y_UP, Y_DN, Y_OP = [(row, at(a, zh) * 2 + core) for a in (yp, ym, yo)]
    H_UP, H_DN, H_OP = [(row, at(y, b) * 2 + core) for b in (hp, hm, ho)]
    L_TO = [(at(x, on(zl, d)), col) for d in (1, 2, 3)]
    SIB = (row, at(y, zh) * 2 + sib)

    locals_ = []

    def local(src, dst):
        copy = pltpu.make_async_copy(src, dst, local_sem.at[len(locals_)])
        locals_.append(copy)
        copy.start()
        return copy

    sent = []

    def send(src, dst, where):
        k = len(sent)
        copy = pltpu.make_async_remote_copy(
            src_ref=src,
            dst_ref=dst,
            send_sem=send_sem.at[k],
            recv_sem=recv_sem.at[k],
            device_id=where,
            device_id_type=MESH,
        )
        copy.start()
        sent.append(copy)
        return copy

    def same(ref, where):
        return send(ref, ref, where)

    own = at(y, zh)
    c_og = local(og_in, grads.at[core, :, own])
    c_wd = local(wd_in, wd_raw)
    c_gp = local(gp_in, gp)
    c_up = local(up_in, up)
    c_wg = local(wg_in, wg_raw)
    c_wu = local(wu_in, wu_raw)
    c_li = local(li_in, inputs.at[core, :, own])

    barrier = pltpu.get_barrier_semaphore()
    partners = [X_UP, X_DN, Y_UP, Y_DN, Y_OP, H_UP, H_DN, H_OP, SIB] + L_TO
    for where in partners:
        pl.semaphore_signal(barrier, inc=1, device_id=where, device_id_type=MESH)
    pl.semaphore_wait(barrier, len(partners))

    def g(block):
        return grads.at[core, :, block]

    def gt(t, block):
        return grads.at[core, t, block]

    TO_H = ((ho, H_OP), (hm, H_UP), (hp, H_DN))
    TO_Y = (Y_OP, Y_UP, Y_DN)
    g_z = [[send(og_in.at[t], gt(t, own), where) for _, where in TO_H] for t in range(PARTS)]
    g_own = [send(og_in, g(own), where) for where in TO_Y]

    def padded(raw, ref, copy):
        copy.wait()
        ref[core, 0:units, :] = raw[...]
        ref[core, units:WIDE, :] = jnp.zeros((WIDE - units, feats), BF)
        return same(ref.at[core], SIB)

    s_wd = padded(wd_raw, wd, c_wd)
    c_gp.wait()
    c_up.wait()
    pre[core] = jnp.zeros((2, 2, 32, WIDE), BF)
    for half in (0, 1):
        pre[core, half, 0, :, 0:units] = gp[half * 32 : half * 32 + 32, :]
        pre[core, half, 1, :, 0:units] = up[half * 32 : half * 32 + 32, :]
    s_pre = same(pre.at[core, sib], SIB)
    for half in (0, 1):
        gate = pre[core, half, 0].astype(F32)
        value = rounded(gate * jax.nn.sigmoid(gate) * pre[core, half, 1].astype(F32))
        hidden[half, :, row] = value.reshape(PARTS, RT, WIDE)

    def h(block):
        return hidden.at[:, :, block]

    hx = [(same(h(row), X_UP), same(h(row), X_DN))]

    g_y = []
    for t in range(PARTS):
        copies = []
        for k in (1, 2, 0):
            g_z[t][k].wait_recv()
            block = gt(t, at(y, TO_H[k][0]))
            copies += [same(block, where) for where in TO_Y]
        g_y.append(copies)

    def li(block):
        return inputs.at[core, :, block]

    i_z = [send(li_in, li(own), where) for _, where in TO_H]
    h_z = [same(h(row), where) for where in L_TO]

    def partial(t, a):
        rows = grads[core, t, pl.ds(a * 4, 4)].reshape(4 * RT, feats)
        for j in (0, 1):
            out = dot(rows, wd[j], NT).reshape(4, RT, WIDE)
            part[t, pl.ds(a * 4, 4), j] = out
            part_bf[t, pl.ds(a * 4, 4), j] = rounded(out)

    def two(ref, t, a, b):
        return ref.at[t, pl.ds(a * 4 + b, 2)]

    def far(t):
        return (
            send(two(part_bf, t, xo, 0), far_lo.at[t], X_UP),
            send(two(part_bf, t, xo, 2), far_hi.at[t], X_DN),
        )

    def early(t):
        return (
            send(two(part_bf, t, xp, 2), from_lo.at[t, pl.ds(2, 2)], X_UP),
            send(two(part_bf, t, xm, 0), from_hi.at[t, pl.ds(0, 2)], X_DN),
        )

    def late(t, arrived):
        arrived[0].wait_recv()
        lo = pl.ds(xp * 4, 2)
        part_bf[t, lo] = rounded(part[t, lo] + far_lo[t].astype(F32))
        up_copy = send(two(part_bf, t, xp, 0), from_lo.at[t, pl.ds(0, 2)], X_UP)
        arrived[1].wait_recv()
        hi = pl.ds(xm * 4 + 2, 2)
        part_bf[t, hi] = rounded(part[t, hi] + far_hi[t].astype(F32))
        return up_copy, send(two(part_bf, t, xm, 2), from_hi.at[t, pl.ds(2, 2)], X_DN)

    def along_z(t, copies):
        for copy in copies:
            copy.wait_recv()

        def x_sum(b):
            return part[t, at(x, b)] + from_lo[t, b].astype(F32) + from_hi[t, b].astype(F32)

        out = []
        for d in (1, 2, 3):
            z_send[t, d - 1] = rounded(x_sum(on(zl, d)))
            out.append(send(z_send.at[t, d - 1], z_recv.at[t, d - 1], L_TO[d - 1]))
        return out, x_sum(zl)

    c_og.wait()
    s_wd.wait_recv()
    for copy in g_own:
        copy.wait_recv()

    def begin(t):
        for copy in g_y[t]:
            copy.wait_recv()
        partial(t, xo)
        first = far(t)
        partial(t, xp)
        partial(t, xm)
        return first

    r0 = begin(0)
    e0 = early(0)
    partial(0, x)
    r1 = begin(1)
    l0 = late(0, r0)
    e1 = early(1)
    partial(1, x)
    l1 = late(1, r1)
    s_g = same(grads.at[core], SIB)
    s_wg = padded(wg_raw, wg, c_wg)
    s_wu = padded(wu_raw, wu, c_wu)

    for copy in i_z:
        copy.wait_recv()
    c_li.wait()
    ref = inputs.at[core, :, pl.ds(y * 4, 4)]
    i_y = [same(ref, where) for where in TO_Y]

    t0, back0 = along_z(0, e0 + l0)
    for d in (1, 2, 3):
        h_z[d - 1].wait_recv()
        block = h(at(x, on(zl, -d)))
        hx.append((same(block, X_UP), same(block, X_DN)))
    t1, back1 = along_z(1, e1 + l1)
    s_pre.wait_recv()

    def b_ref(t, a, b):
        return backs.at[t, at(a, b)]

    def start_backs(t, back, copies):
        for d in (1, 2, 3):
            copies[d - 1].wait_recv()
            back = back + z_recv[t, d - 1].astype(F32)
        for j in (0, 1):
            rows = pl.ds(t * RT, RT)
            gate = pre[j, core, 0, rows].astype(F32)
            upper = pre[j, core, 1, rows].astype(F32)
            sig = jax.nn.sigmoid(gate)
            backs[t, row, 0, j] = rounded(back[j] * upper * sig * (1.0 + gate * (1.0 - sig)))
            backs[t, row, 1, j] = rounded(back[j] * gate * sig)
        ref = backs.at[t, row]
        return [same(ref, X_UP)], [same(ref, X_DN)], [same(ref, where) for where in L_TO]

    bu0, bd0, bz0 = start_backs(0, back0, t0)
    bu1, bd1, bz1 = start_backs(1, back1, t1)

    for copy in i_y:
        copy.wait_recv()
    s_i = same(inputs.at[core], SIB)

    def from_z(t, bu, bd, bz, d):
        bz[d - 1].wait_recv()
        ref = b_ref(t, x, on(zl, -d))
        bu.append(same(ref, X_UP))
        bd.append(same(ref, X_DN))

    def forward(t, copy, a, b, where):
        copy.wait_recv()
        return same(b_ref(t, a, b), where)

    s_b = []

    def use(t, a):
        total = None
        for k, weight in ((0, wg), (1, wu)):
            for j in (0, 1):
                rows = backs[t, pl.ds(a * 4, 4), k, j].reshape(4 * RT, WIDE)
                term = dot(rows, weight[j], NN)
                total = term if total is None else total + term
        out = total.reshape(4, RT, feats)
        iq[t, pl.ds(a * 4, 4)] = out
        iq_bf[t, pl.ds(a * 4, 4)] = rounded(out)
        some = pl.ds(a * 4, 4)
        s_b.append(send(backs.at[t, some, :, sib], backs_sib.at[t, some], SIB))

    def plane(ref, t, a):
        return ref.at[t, pl.ds(a * 4, 4)]

    def along_y(t):
        return [
            send(plane(iq_bf, t, a), i_recv.at[t, k], where)
            for k, (a, where) in enumerate(((yo, Y_OP), (yp, Y_UP), (ym, Y_DN)))
        ]

    def along_h(t, copies):
        for copy in copies:
            copy.wait_recv()

        def y_sum(b):
            out = iq[t, at(y, b)]
            for k in range(3):
                out = out + i_recv[t, k, b].astype(F32)
            return out

        out = []
        for k, (b, where) in enumerate(((ho, H_OP), (hp, H_UP), (hm, H_DN))):
            iz_send[t, k] = rounded(y_sum(b))
            out.append(send(iz_send.at[t, k], iz_recv.at[t, k], where))
        return out, y_sum(zh)

    def finish(t, copies, total):
        for k in range(3):
            copies[k].wait_recv()
            total = total + iz_recv[t, k].astype(F32)
        ig[t] = rounded(total)

    bf0, bf1 = [], []
    from_z(0, bu0, bd0, bz0, 1)
    bf0.append(forward(0, bu0[0], xm, zl, X_UP))
    from_z(0, bu0, bd0, bz0, 2)
    bf1.append(forward(1, bu1[0], xm, zl, X_UP))
    from_z(0, bu0, bd0, bz0, 3)
    s_wg.wait_recv()
    s_wu.wait_recv()
    use(0, x)
    bf0.append(forward(0, bd0[1], xp, on(zl, -1), X_DN))
    from_z(1, bu1, bd1, bz1, 1)
    bf0.append(forward(0, bu0[2], xm, on(zl, -2), X_UP))
    from_z(1, bu1, bd1, bz1, 2)
    bf0.append(forward(0, bd0[3], xp, on(zl, -3), X_DN))
    from_z(1, bu1, bd1, bz1, 3)
    bu0[1].wait_recv()
    bu0[3].wait_recv()
    use(0, xm)
    bf1.append(forward(1, bd1[1], xp, on(zl, -1), X_DN))
    bd0[0].wait_recv()
    bd0[2].wait_recv()
    use(0, xp)
    bf1.append(forward(1, bu1[2], xm, on(zl, -2), X_UP))
    use(1, x)
    for copy in bf0:
        copy.wait_recv()
    use(0, xo)
    q0 = along_y(0)
    bf1.append(forward(1, bd1[3], xp, on(zl, -3), X_DN))

    for k in range(4):
        hx[k][0].wait_recv()
        hx[k][1].wait_recv()
    hf = [
        same(h(at(xm, zl)), X_UP),
        same(h(at(xm, on(zl, -1))), X_UP),
        same(h(at(xp, on(zl, -2))), X_DN),
        same(h(at(xp, on(zl, -3))), X_DN),
    ]

    bu1[1].wait_recv()
    bu1[3].wait_recv()
    use(1, xm)
    bd1[0].wait_recv()
    bd1[2].wait_recv()
    use(1, xp)
    z0, total0 = along_h(0, q0)
    for copy in bf1:
        copy.wait_recv()
    use(1, xo)
    q1 = along_y(1)

    def tokens(value):
        return value.reshape(512, value.shape[-1])

    for copy in hf:
        copy.wait_recv()
    s_g.wait_recv()
    dg[...] = rounded(
        dot(hidden[...].reshape(1024, WIDE), grads[...].reshape(1024, feats), TN)[0:units, :]
    )
    outs = [local(dg, dg_out)]
    z1, total1 = along_h(1, q1)
    finish(0, z0, total0)
    s_i.wait_recv()
    for copy in s_b:
        copy.wait_recv()
    for k, ref, out in ((0, gg, gg_out), (1, ug, ug_out)):
        value = dot(tokens(backs[:, :, k, core]), tokens(inputs[core]), TN)
        value = value + dot(tokens(backs_sib[:, :, k]), tokens(inputs[sib]), TN)
        ref[...] = rounded(value[0:units, :])
        outs.append(local(ref, out))
    finish(1, z1, total1)
    outs.append(local(ig, ig_out))

    for copy in sent:
        copy.wait_send()
    for copy in outs:
        copy.wait()


def hand_over(*refs):
    sources, targets, rooms, sem = refs[:4], refs[4:8], refs[8:12], refs[12]
    into = [pltpu.make_async_copy(s, v, sem.at[k]) for k, (s, v) in enumerate(zip(sources, rooms))]
    out = [pltpu.make_async_copy(v, t, sem.at[4 + k]) for k, (v, t) in enumerate(zip(rooms, targets))]
    for copy in into:
        copy.start()
    for first, second in zip(into, out):
        first.wait()
        second.start()
    for copy in out:
        copy.wait()


def shards(out_grad, layer_input, gate_preact, up_preact, w_down, w_gate, w_up):
    tokens, feats = out_grad.shape
    units = gate_preact.shape[1]
    vm = pltpu.VMEM
    any_space = pl.BlockSpec(memory_space=pl.ANY)
    shapes = (
        jax.ShapeDtypeStruct((PARTS, RT, feats), BF),
        jax.ShapeDtypeStruct((units, feats), BF),
        jax.ShapeDtypeStruct((units, feats), BF),
        jax.ShapeDtypeStruct((units, feats), BF),
    )
    results = pl.pallas_call(
        kernel,
        out_shape=shapes,
        in_specs=[any_space] * 7,
        out_specs=(any_space,) * 4,
        scratch_shapes=[
            vm((2, PARTS, 16, RT, feats), BF),
            vm((2, PARTS, 16, RT, feats), BF),
            vm((2, PARTS, 16, RT, WIDE), BF),
            vm((PARTS, 16, 2, 2, RT, WIDE), BF),
            vm((PARTS, 16, 2, RT, WIDE), BF),
            vm((64, units), BF), vm((64, units), BF), vm((2, 2, 2, 32, WIDE), BF),
            vm((units, feats), BF), vm((units, feats), BF), vm((units, feats), BF),
            vm((2, WIDE, feats), BF), vm((2, WIDE, feats), BF), vm((2, WIDE, feats), BF),
            vm((PARTS, 16, 2, RT, WIDE), F32), vm((PARTS, 16, 2, RT, WIDE), BF),
            vm((PARTS, 2, 2, RT, WIDE), BF), vm((PARTS, 2, 2, RT, WIDE), BF),
            vm((PARTS, 4, 2, RT, WIDE), BF), vm((PARTS, 4, 2, RT, WIDE), BF),
            vm((PARTS, 3, 2, RT, WIDE), BF), vm((PARTS, 3, 2, RT, WIDE), BF),
            vm((PARTS, 16, RT, feats), F32), vm((PARTS, 16, RT, feats), BF),
            vm((PARTS, 3, 4, RT, feats), BF),
            vm((PARTS, 3, RT, feats), BF), vm((PARTS, 3, RT, feats), BF),
            vm((units, feats), BF), vm((units, feats), BF), vm((units, feats), BF),
            vm((PARTS, RT, feats), BF),
            pltpu.SemaphoreType.DMA((16,)),
            pltpu.SemaphoreType.DMA((N_COPIES,)),
            pltpu.SemaphoreType.DMA((N_COPIES,)),
        ],
        compiler_params=pltpu.CompilerParams(
            collective_id=0, has_side_effects=True, vmem_limit_bytes=VMEM_ALL
        ),
        cost_estimate=pl.CostEstimate(
            flops=12 * 1024 * units * feats, bytes_accessed=3_000_000, transcendentals=64 * units
        ),
        name="swiglu_back",
    )(
        out_grad.reshape(PARTS, RT, feats),
        layer_input.reshape(PARTS, RT, feats),
        gate_preact,
        up_preact,
        w_down.T,
        w_gate,
        w_up,
    )
    ig, dg, gg, ug = pl.pallas_call(
        hand_over,
        out_shape=shapes,
        in_specs=[any_space] * 4,
        out_specs=(any_space,) * 4,
        scratch_shapes=[vm(s.shape, s.dtype) for s in shapes] + [pltpu.SemaphoreType.DMA((8,))],
        compiler_params=pltpu.CompilerParams(vmem_limit_bytes=VMEM_ALL),
        name="hand_over",
    )(*results)
    return ig.reshape(tokens, feats), dg.T, gg, ug


def solution(mesh):
    return jax.shard_map(
        shards,
        mesh=mesh,
        in_specs=(
            P("col", "row"),
            P("col", "row"),
            P("row", "col"),
            P("row", "col"),
            P("row", "col"),
            P("col", "row"),
            P("col", "row"),
        ),
        out_specs=(P("col", "row"), P("row", "col"), P("col", "row"), P("col", "row")),
        check_vma=False,
    )
```

time: 416 us -> 87.1 us (0.21)
  the two profiles are of different devices: /device:TPU:24 before, /device:TPU:2 now
where the time goes in v2:
time: 87.1 us; the launch traced here: 86.9 us
  Pallas kernels  86.3 us (99%)
    pallas_call x1, Pallas kernels, shards(): pl.pallas_call(kernel, out_shape=shapes, in_specs=[any_space] * 7, out_sp...  84.1 us
    pallas_call x1, Pallas kernels, shards(): pl.pallas_call(hand_over, out_shape=shapes, in_specs=[any_space] * 4, out...  2.2 us

profile of v2, /device:TPU:2, one launch (start us, length us, event | category | flops | bytes accessed | tf_op | source)
XLA Modules:
  0.0 86.9 jit_solution(9334313755593809422)
XLA Ops:
  0.6 84.1 %swiglu_back.1 = (bf16[2,16,512]{2,1,0:T(8,128)(2,1)}, bf16[462,512]{1,0:T(8,128)(2,1)}, bf16[462,512]{1,0:T(8,128)(2,1)}, bf16[462,512]{1,0:T(8,128)(2,1)}) custom-call(bf16[2,16,512]{2,1,0:T(8,128)(2,1)} %bitcast.7, bf16[2,16,512]{2,1,0:T(8,128)(2,1)} %bitcast.8, bf16[64,462]{1,0:T(8,128)(2,1)} %gp_in.1, bf16[64,462]{1,0:T(8,128)(2,1)} %up_in.1, ...), custom_call_target="tpu_custom_call" | custom-call | flops 2906652672 | bytes 3000000 | tf_op jit(solution)/shard_map/swiglu_back/pallas_call | solution.py:426
  84.7 2.2 %hand_over.1 = (bf16[2,16,512]{2,1,0:T(8,128)(2,1)}, bf16[462,512]{1,0:T(8,128)(2,1)}, bf16[462,512]{1,0:T(8,128)(2,1)}, bf16[462,512]{1,0:T(8,128)(2,1)}) custom-call(bf16[2,16,512]{2,1,0:T(8,128)(2,1)} %get-tuple-element.12.refs_0_, bf16[462,512]{1,0:T(8,128)(2,1)} %get-tuple-element.13.refs_1_, bf16[462,512]{1,0:T(8,128)(2,1)} %get-tuple-element.14.refs_2_, ...), custom_call_target="tpu_custom_call" | custom-call | tf_op jit(solution)/shard_map/hand_over/pallas_call | solution.py:469

commit v3 on v2

v3 whole, which is shorter than its diff:
```python
import jax
import jax.numpy as jnp
from jax import lax
from jax.experimental import pallas as pl
from jax.experimental.pallas import tpu as pltpu
from jax.sharding import PartitionSpec as P

BF = jnp.bfloat16
F32 = jnp.float32
MESH = pl.DeviceIdType.MESH
N_GROUPS = 7
N_ARRIVALS = 60
WIDE = 512
PARTS = 2
RT = 32 // PARTS
VMEM_ALL = 64 * 1024 * 1024 - 65536


def rounded(value):
    return value.astype(BF)


def dot(left, right, dims):
    return lax.dot_general(left, right, (dims, ((), ())), preferred_element_type=F32)


NN = ((1,), (0,))
NT = ((1,), (1,))
TN = ((0,), (0,))


def kernel(
    og_in, li_in, gp_in, up_in, wd_in, wg_in, wu_in,
    ig_out, dg_out, gg_out, ug_out,
    grads, inputs, hidden, backs, backs_sib,
    gp, up, pre, wd_raw, wg_raw, wu_raw, wd, wg, wu,
    part, part_bf, far_lo, far_hi, from_lo, from_hi, z_send, z_recv,
    iq, iq_bf, i_recv, iz_send, iz_recv,
    gg, ug, dg, ig,
    local_sem, send_sem, recv_sem,
):
    units = gp_in.shape[1]
    feats = og_in.shape[2]
    row, col = lax.axis_index("row"), lax.axis_index("col")
    x, zl = lax.div(row, 4), lax.rem(row, 4)
    y, zh, core = lax.div(col, 8), lax.rem(lax.div(col, 2), 4), lax.rem(col, 2)
    sib = 1 - core

    def on(value, step):
        return lax.rem(value + step + 4, 4)

    xp, xm, xo = on(x, 1), on(x, -1), on(x, 2)
    yp, ym, yo = on(y, 1), on(y, -1), on(y, 2)
    hp, hm, ho = on(zh, 1), on(zh, -1), on(zh, 2)

    def at(a, b):
        return a * 4 + b

    X_UP, X_DN, X_OP = [(at(a, zl), col) for a in (xp, xm, xo)]
    Y_UP, Y_DN, Y_OP = [(row, at(a, zh) * 2 + core) for a in (yp, ym, yo)]
    H_UP, H_DN, H_OP = [(row, at(y, b) * 2 + core) for b in (hp, hm, ho)]
    L_TO = [(at(x, on(zl, d)), col) for d in (1, 2, 3)]
    SIB = (row, at(y, zh) * 2 + sib)

    locals_ = []

    def local(src, dst):
        copy = pltpu.make_async_copy(src, dst, local_sem.at[len(locals_)])
        locals_.append(copy)
        copy.start()
        return copy

    arrivals = []

    def arrival():
        arrivals.append(recv_sem.at[len(arrivals)])
        return arrivals[-1]

    def remote(src, dst, where, group, arrived):
        return pltpu.make_async_remote_copy(
            src_ref=src,
            dst_ref=dst,
            send_sem=send_sem.at[group],
            recv_sem=arrived,
            device_id=where,
            device_id_type=MESH,
        )

    def send(src, dst, where, group, arrived):
        remote(src, dst, where, group, arrived).start()

    def same(ref, where, group, arrived):
        remote(ref, ref, where, group, arrived).start()

    def wait(arrived, like):
        remote(like, like, SIB, 0, arrived).wait_recv()

    def wait_sent(group, like):
        remote(like, like, SIB, group, arrivals[0]).wait_send()

    OUT_A, OUT_W, OUT_H, OUT_B, OUT_C, OUT_S, OUT_D = range(N_GROUPS)

    own = at(y, zh)
    c_og = local(og_in, grads.at[core, :, own])
    c_wd = local(wd_in, wd_raw)
    c_gp = local(gp_in, gp)
    c_up = local(up_in, up)
    c_wg = local(wg_in, wg_raw)
    c_wu = local(wu_in, wu_raw)
    c_li = local(li_in, inputs.at[core, :, own])

    barrier = pltpu.get_barrier_semaphore()
    partners = [X_UP, X_DN, X_OP, Y_UP, Y_DN, Y_OP, H_UP, H_DN, H_OP, SIB] + L_TO
    for where in partners:
        pl.semaphore_signal(barrier, inc=1, device_id=where, device_id_type=MESH)
    pl.semaphore_wait(barrier, len(partners))

    def g(block):
        return grads.at[core, :, block]

    def gt(t, block):
        return grads.at[core, t, block]

    TO_H = ((ho, H_OP), (hm, H_UP), (hp, H_DN))
    TO_Y = (Y_OP, Y_UP, Y_DN)
    g_z = [[arrival() for _ in range(3)] for _ in range(PARTS)]
    g_own = arrival()
    for t in range(PARTS):
        for k in range(3):
            send(og_in.at[t], gt(t, own), TO_H[k][1], OUT_A, g_z[t][k])
    for where in TO_Y:
        send(og_in, g(own), where, OUT_A, g_own)

    def padded(raw, ref, copy):
        copy.wait()
        ref[core, 0:units, :] = raw[...]
        ref[core, units:WIDE, :] = jnp.zeros((WIDE - units, feats), BF)
        arrived = arrival()
        same(ref.at[core], SIB, OUT_W, arrived)
        return arrived

    s_wd = padded(wd_raw, wd, c_wd)
    c_gp.wait()
    c_up.wait()
    pre[core] = jnp.zeros((2, 2, 32, WIDE), BF)
    for half in (0, 1):
        pre[core, half, 0, :, 0:units] = gp[half * 32 : half * 32 + 32, :]
        pre[core, half, 1, :, 0:units] = up[half * 32 : half * 32 + 32, :]
    s_pre = arrival()
    same(pre.at[core, sib], SIB, OUT_H, s_pre)
    for half in (0, 1):
        gate = pre[core, half, 0].astype(F32)
        value = rounded(gate * jax.nn.sigmoid(gate) * pre[core, half, 1].astype(F32))
        hidden[half, :, row] = value.reshape(PARTS, RT, WIDE)

    def h(block):
        return hidden.at[:, :, block]

    h_x, h_z = arrival(), arrival()
    for where in (X_OP, X_UP, X_DN):
        same(h(row), where, OUT_H, h_x)

    g_y = [arrival() for _ in range(PARTS)]
    for t in range(PARTS):
        for k in (1, 2, 0):
            block = gt(t, at(y, TO_H[k][0]))
            wait(g_z[t][k], block)
            for where in TO_Y:
                same(block, where, OUT_A, g_y[t])

    def li(block):
        return inputs.at[core, :, block]

    i_z = arrival()
    for _, where in TO_H:
        send(li_in, li(own), where, OUT_A, i_z)

    def partial(t, j):
        rows = grads[core, t].reshape(16 * RT, feats)
        out = dot(rows, wd[j], NT).reshape(16, RT, WIDE)
        part[t * 2 + j] = out
        part_bf[t * 2 + j] = rounded(out)

    def two(ref, u, a, b):
        return ref.at[u, pl.ds(a * 4 + b, 2)]

    n_units = 2 * PARTS
    r_up = [arrival() for _ in range(n_units)]
    r_dn = [arrival() for _ in range(n_units)]
    x_in = [arrival() for _ in range(n_units)]
    z_in = [arrival() for _ in range(n_units)]

    def begin(u):
        send(two(part_bf, u, xo, 0), far_lo.at[u], X_UP, OUT_B, r_up[u])
        send(two(part_bf, u, xo, 2), far_hi.at[u], X_DN, OUT_B, r_dn[u])
        send(two(part_bf, u, xp, 2), from_lo.at[u, pl.ds(2, 2)], X_UP, OUT_B, x_in[u])
        send(two(part_bf, u, xm, 0), from_hi.at[u, pl.ds(0, 2)], X_DN, OUT_B, x_in[u])

    def late(u):
        wait(r_up[u], far_lo.at[u])
        lo = pl.ds(xp * 4, 2)
        part_bf[u, lo] = rounded(part[u, lo] + far_lo[u].astype(F32))
        send(two(part_bf, u, xp, 0), from_lo.at[u, pl.ds(0, 2)], X_UP, OUT_B, x_in[u])
        wait(r_dn[u], far_hi.at[u])
        hi = pl.ds(xm * 4 + 2, 2)
        part_bf[u, hi] = rounded(part[u, hi] + far_hi[u].astype(F32))
        send(two(part_bf, u, xm, 2), from_hi.at[u, pl.ds(2, 2)], X_DN, OUT_B, x_in[u])

    def x_sum(u, b):
        return part[u, at(x, b)] + from_lo[u, b].astype(F32) + from_hi[u, b].astype(F32)

    def along_z(u):
        wait(x_in[u], part_bf.at[u, pl.ds(0, 8)])
        for d in (2, 1, 3):
            z_send[u, d - 1] = rounded(x_sum(u, on(zl, d)))
            send(z_send.at[u, d - 1], z_recv.at[u, d - 1], L_TO[d - 1], OUT_B, z_in[u])

    c_og.wait()
    wait(s_wd, wd.at[sib])
    wait(g_own, grads.at[0, :, pl.ds(0, 3)])
    wait(g_y[0], grads.at[0, 0, pl.ds(0, 9)])
    partial(0, 0)
    begin(0)
    partial(0, 1)
    begin(1)
    late(0)
    wait(g_y[1], grads.at[0, 0, pl.ds(0, 9)])
    partial(1, 0)
    begin(2)
    late(1)
    partial(1, 1)
    begin(3)
    along_z(0)
    late(2)
    along_z(1)
    late(3)
    s_g = arrival()
    same(grads.at[core], SIB, OUT_W, s_g)
    s_wg = padded(wg_raw, wg, c_wg)
    s_wu = padded(wu_raw, wu, c_wu)
    along_z(2)

    along_z(3)
    wait(s_pre, pre.at[sib, core])

    def b_ref(t, a, b):
        return backs.at[t, at(a, b)]

    b_z = [[arrival() for _ in range(3)] for _ in range(PARTS)]
    b_one = [[arrival() for _ in range(4)] for _ in range(PARTS)]
    b_up = [arrival() for _ in range(PARTS)]
    b_dn = [arrival() for _ in range(PARTS)]
    b_far = [arrival() for _ in range(PARTS)]

    def backs_x(t, d):
        ref = b_ref(t, x, on(zl, -d))
        same(ref, X_UP, OUT_C, {2: b_one[t][0], 3: b_one[t][1]}.get(d, b_up[t]))
        same(ref, X_DN, OUT_C, {1: b_one[t][2], 3: b_one[t][3]}.get(d, b_dn[t]))

    def start_backs(t):
        for j in (0, 1):
            u = t * 2 + j
            wait(z_in[u], z_recv.at[u])
            back = x_sum(u, zl)
            for d in (1, 2, 3):
                back = back + z_recv[u, d - 1].astype(F32)
            rows = pl.ds(t * RT, RT)
            gate = pre[j, core, 0, rows].astype(F32)
            upper = pre[j, core, 1, rows].astype(F32)
            sig = jax.nn.sigmoid(gate)
            backs[t, row, 0, j] = rounded(back * upper * sig * (1.0 + gate * (1.0 - sig)))
            backs[t, row, 1, j] = rounded(back * gate * sig)
        for d in (2, 1, 3):
            same(backs.at[t, row], L_TO[d - 1], OUT_C, b_z[t][d - 1])
        same(backs.at[t, row], X_OP, OUT_C, b_far[t])
        backs_x(t, 0)

    start_backs(0)

    wait(i_z, inputs.at[0, :, pl.ds(0, 3)])
    c_li.wait()
    i_y = arrival()
    for where in TO_Y:
        same(inputs.at[core, :, pl.ds(y * 4, 4)], where, OUT_H, i_y)
    start_backs(1)

    def from_z(t, d):
        wait(b_z[t][d - 1], b_ref(t, x, on(zl, -d)))
        backs_x(t, d)

    def forward(t, d):
        up_ref, dn_ref = b_ref(t, xm, on(zl, -d)), b_ref(t, xp, on(zl, -d))
        if d == 2:
            wait(b_one[t][0], up_ref)
            same(up_ref, X_UP, OUT_C, b_far[t])
        elif d == 1:
            wait(b_one[t][2], dn_ref)
            same(dn_ref, X_DN, OUT_C, b_far[t])
        else:
            wait(b_one[t][1], up_ref)
            same(up_ref.at[0], X_UP, OUT_C, b_far[t])
            wait(b_one[t][3], dn_ref)
            same(dn_ref.at[1], X_DN, OUT_C, b_far[t])

    s_b = arrival()
    q_y = [arrival() for _ in range(PARTS)]
    q_z = [arrival() for _ in range(PARTS)]

    def to_y(t, a):
        @pl.when(a != y)
        def _():
            where = (row, at(a, zh) * 2 + core)
            send(iq_bf.at[t, pl.ds(a * 4, 4)], i_recv.at[t, y], where, OUT_D, q_y[t])

    def use(t, planes):
        total = None
        for k, weight in ((0, wg), (1, wu)):
            for j in (0, 1):
                rows = [backs[t, pl.ds(a * 4, 4), k, j].reshape(4 * RT, WIDE) for a in planes]
                rows = rows[0] if len(rows) == 1 else jnp.concatenate(rows, axis=0)
                term = dot(rows, weight[j], NN)
                total = term if total is None else total + term
        for k, a in enumerate(planes):
            out = total[k * 4 * RT : (k + 1) * 4 * RT].reshape(4, RT, feats)
            some = pl.ds(a * 4, 4)
            iq[t, some] = out
            iq_bf[t, some] = rounded(out)
            to_y(t, a)
            send(backs.at[t, some, :, sib], backs_sib.at[t, some], SIB, OUT_S, s_b)

    def y_sum(t, b):
        out = iq[t, at(y, b)]
        for k in range(3):
            out = out + i_recv[t, on(y, k + 1), b].astype(F32)
        return out

    def along_h(t):
        wait(q_y[t], i_recv.at[t, pl.ds(0, 3)])
        for k, (b, where) in enumerate(((ho, H_OP), (hp, H_UP), (hm, H_DN))):
            iz_send[t, k] = rounded(y_sum(t, b))
            send(iz_send.at[t, k], iz_recv.at[t, k], where, OUT_D, q_z[t])

    def finish(t):
        wait(q_z[t], iz_recv.at[t])
        total = y_sum(t, zh)
        for k in range(3):
            total = total + iz_recv[t, k].astype(F32)
        ig[t] = rounded(total)

    for t in range(PARTS):
        for d in (2, 1, 3):
            from_z(t, d)

    for where in L_TO:
        same(h(row), where, OUT_H, h_z)
    wait(s_wg, wg.at[sib])
    wait(s_wu, wu.at[sib])
    forward(0, 2)
    forward(0, 1)
    forward(0, 3)
    forward(1, 2)
    wait(b_up[0], backs.at[0, pl.ds(0, 2)])
    wait(b_dn[0], backs.at[0, pl.ds(0, 2)])
    use(0, (x, xm, xp))
    forward(1, 1)
    forward(1, 3)
    wait(b_far[0], backs.at[0, pl.ds(0, 4)])
    use(0, (xo,))
    wait(h_z, hidden.at[:, :, pl.ds(0, 3)])
    for d in (1, 2, 3):
        for where in (X_OP, X_UP, X_DN):
            same(h(at(x, on(zl, -d))), where, OUT_H, h_x)
    wait(i_y, inputs.at[0, :, pl.ds(0, 12)])
    s_i = arrival()
    same(inputs.at[core], SIB, OUT_H, s_i)

    wait(b_up[1], backs.at[1, pl.ds(0, 2)])
    wait(b_dn[1], backs.at[1, pl.ds(0, 2)])
    use(1, (x, xm, xp))
    along_h(0)
    wait(b_far[1], backs.at[1, pl.ds(0, 4)])
    use(1, (xo,))
    along_h(1)

    def tokens(value):
        return value.reshape(512, value.shape[-1])

    wait(s_i, inputs.at[sib])
    wait(s_b, backs_sib)
    outs = []
    for k, ref, out in ((0, gg, gg_out), (1, ug, ug_out)):
        value = dot(tokens(backs[:, :, k, core]), tokens(inputs[core]), TN)
        value = value + dot(tokens(backs_sib[:, :, k]), tokens(inputs[sib]), TN)
        ref[...] = rounded(value[0:units, :])
        outs.append(local(ref, out))
    finish(0)
    wait(h_x, hidden.at[:, :, pl.ds(0, 12)])
    wait(s_g, grads.at[sib])
    dg[...] = rounded(
        dot(hidden[...].reshape(1024, WIDE), grads[...].reshape(1024, feats), TN)[0:units, :]
    )
    outs.append(local(dg, dg_out))
    finish(1)
    outs.append(local(ig, ig_out))

    wait_sent(OUT_A, grads.at[:, :, pl.ds(0, 9)])
    wait_sent(OUT_W, backs)
    wait_sent(OUT_H, backs.at[:, pl.ds(0, 15)])
    wait_sent(OUT_B, grads.at[:, :, pl.ds(0, 15)])
    wait_sent(OUT_C, backs.at[:, pl.ds(0, 15)])
    wait_sent(OUT_S, backs.at[0])
    wait_sent(OUT_D, grads.at[0, :, pl.ds(0, 15)])
    for copy in outs:
        copy.wait()
    assert len(arrivals) == N_ARRIVALS, len(arrivals)


def hand_over(*refs):
    sources, targets, rooms, sem = refs[:4], refs[4:8], refs[8:12], refs[12]
    into = [pltpu.make_async_copy(s, v, sem.at[k]) for k, (s, v) in enumerate(zip(sources, rooms))]
    out = [pltpu.make_async_copy(v, t, sem.at[4 + k]) for k, (v, t) in enumerate(zip(rooms, targets))]
    for copy in into:
        copy.start()
    for first, second in zip(into, out):
        first.wait()
        second.start()
    for copy in out:
        copy.wait()


def shards(out_grad, layer_input, gate_preact, up_preact, w_down, w_gate, w_up):
    tokens, feats = out_grad.shape
    units = gate_preact.shape[1]
    vm = pltpu.VMEM
    any_space = pl.BlockSpec(memory_space=pl.ANY)
    shapes = (
        jax.ShapeDtypeStruct((PARTS, RT, feats), BF),
        jax.ShapeDtypeStruct((units, feats), BF),
        jax.ShapeDtypeStruct((units, feats), BF),
        jax.ShapeDtypeStruct((units, feats), BF),
    )
    results = pl.pallas_call(
        kernel,
        out_shape=shapes,
        in_specs=[any_space] * 7,
        out_specs=(any_space,) * 4,
        scratch_shapes=[
            vm((2, PARTS, 16, RT, feats), BF),
            vm((2, PARTS, 16, RT, feats), BF),
            vm((2, PARTS, 16, RT, WIDE), BF),
            vm((PARTS, 16, 2, 2, RT, WIDE), BF),
            vm((PARTS, 16, 2, RT, WIDE), BF),
            vm((64, units), BF), vm((64, units), BF), vm((2, 2, 2, 32, WIDE), BF),
            vm((units, feats), BF), vm((units, feats), BF), vm((units, feats), BF),
            vm((2, WIDE, feats), BF), vm((2, WIDE, feats), BF), vm((2, WIDE, feats), BF),
            vm((2 * PARTS, 16, RT, WIDE), F32), vm((2 * PARTS, 16, RT, WIDE), BF),
            vm((2 * PARTS, 2, RT, WIDE), BF), vm((2 * PARTS, 2, RT, WIDE), BF),
            vm((2 * PARTS, 4, RT, WIDE), BF), vm((2 * PARTS, 4, RT, WIDE), BF),
            vm((2 * PARTS, 3, RT, WIDE), BF), vm((2 * PARTS, 3, RT, WIDE), BF),
            vm((PARTS, 16, RT, feats), F32), vm((PARTS, 16, RT, feats), BF),
            vm((PARTS, 4, 4, RT, feats), BF),
            vm((PARTS, 3, RT, feats), BF), vm((PARTS, 3, RT, feats), BF),
            vm((units, feats), BF), vm((units, feats), BF), vm((units, feats), BF),
            vm((PARTS, RT, feats), BF),
            pltpu.SemaphoreType.DMA((11,)),
            pltpu.SemaphoreType.DMA((N_GROUPS,)),
            pltpu.SemaphoreType.DMA((N_ARRIVALS,)),
        ],
        compiler_params=pltpu.CompilerParams(
            collective_id=0, has_side_effects=True, vmem_limit_bytes=VMEM_ALL
        ),
        cost_estimate=pl.CostEstimate(
            flops=12 * 1024 * units * feats, bytes_accessed=3_000_000, transcendentals=64 * units
        ),
        name="swiglu_back",
    )(
        out_grad.reshape(PARTS, RT, feats),
        layer_input.reshape(PARTS, RT, feats),
        gate_preact,
        up_preact,
        w_down.T,
        w_gate,
        w_up,
    )
    ig, dg, gg, ug = pl.pallas_call(
        hand_over,
        out_shape=shapes,
        in_specs=[any_space] * 4,
        out_specs=(any_space,) * 4,
        scratch_shapes=[vm(s.shape, s.dtype) for s in shapes] + [pltpu.SemaphoreType.DMA((8,))],
        compiler_params=pltpu.CompilerParams(vmem_limit_bytes=VMEM_ALL),
        name="hand_over",
    )(*results)
    return ig.reshape(tokens, feats), dg.T, gg, ug


def solution(mesh):
    return jax.shard_map(
        shards,
        mesh=mesh,
        in_specs=(
            P("col", "row"),
            P("col", "row"),
            P("row", "col"),
            P("row", "col"),
            P("row", "col"),
            P("col", "row"),
            P("col", "row"),
        ),
        out_specs=(P("col", "row"), P("row", "col"), P("col", "row"), P("col", "row")),
        check_vma=False,
    )
```

time: 87.1 us -> 84.1 us (0.966)
  the two profiles are of different devices: /device:TPU:2 before, /device:TPU:24 now
where the time goes in v3:
time: 84.1 us; the launch traced here: 82.8 us
  Pallas kernels  82.1 us (98%)
    pallas_call x1, Pallas kernels, shards(): pl.pallas_call(kernel, out_shape=shapes, in_specs=[any_space] * 7, out_sp...  79.9 us
    pallas_call x1, Pallas kernels, shards(): pl.pallas_call(hand_over, out_shape=shapes, in_specs=[any_space] * 4, out...  2.2 us

profile of v3, /device:TPU:24, one launch (start us, length us, event | category | flops | bytes accessed | tf_op | source)
XLA Modules:
  0.0 82.8 jit_solution(5954692871236805971)
XLA Ops:
  0.6 79.9 %swiglu_back.1 = (bf16[2,16,512]{2,1,0:T(8,128)(2,1)}, bf16[462,512]{1,0:T(8,128)(2,1)}, bf16[462,512]{1,0:T(8,128)(2,1)}, bf16[462,512]{1,0:T(8,128)(2,1)}) custom-call(bf16[2,16,512]{2,1,0:T(8,128)(2,1)} %bitcast.7, bf16[2,16,512]{2,1,0:T(8,128)(2,1)} %bitcast.8, bf16[64,462]{1,0:T(8,128)(2,1)} %gp_in.1, bf16[64,462]{1,0:T(8,128)(2,1)} %up_in.1, ...), custom_call_target="tpu_custom_call" | custom-call | flops 2906652672 | bytes 3000000 | tf_op jit(solution)/shard_map/swiglu_back/pallas_call | solution.py:442
  80.6 2.2 %hand_over.1 = (bf16[2,16,512]{2,1,0:T(8,128)(2,1)}, bf16[462,512]{1,0:T(8,128)(2,1)}, bf16[462,512]{1,0:T(8,128)(2,1)}, bf16[462,512]{1,0:T(8,128)(2,1)}) custom-call(bf16[2,16,512]{2,1,0:T(8,128)(2,1)} %get-tuple-element.12.refs_0_, bf16[462,512]{1,0:T(8,128)(2,1)} %get-tuple-element.13.refs_1_, bf16[462,512]{1,0:T(8,128)(2,1)} %get-tuple-element.14.refs_2_, ...), custom_call_target="tpu_custom_call" | custom-call | tf_op jit(solution)/shard_map/hand_over/pallas_call | solution.py:485

commit v4 on v3

--- a/solution.py
+++ b/solution.py
@@ -252,11 +252,6 @@
     b_dn = [arrival() for _ in range(PARTS)]
     b_far = [arrival() for _ in range(PARTS)]
 
-    def backs_x(t, d):
-        ref = b_ref(t, x, on(zl, -d))
-        same(ref, X_UP, OUT_C, {2: b_one[t][0], 3: b_one[t][1]}.get(d, b_up[t]))
-        same(ref, X_DN, OUT_C, {1: b_one[t][2], 3: b_one[t][3]}.get(d, b_dn[t]))
-
     def start_backs(t):
         for j in (0, 1):
             u = t * 2 + j
@@ -273,7 +268,8 @@
         for d in (2, 1, 3):
             same(backs.at[t, row], L_TO[d - 1], OUT_C, b_z[t][d - 1])
         same(backs.at[t, row], X_OP, OUT_C, b_far[t])
-        backs_x(t, 0)
+        same(backs.at[t, row], X_UP, OUT_C, b_up[t])
+        same(backs.at[t, row], X_DN, OUT_C, b_dn[t])
 
     start_backs(0)
 
@@ -285,8 +281,16 @@
     start_backs(1)
 
     def from_z(t, d):
-        wait(b_z[t][d - 1], b_ref(t, x, on(zl, -d)))
-        backs_x(t, d)
+        ref = b_ref(t, x, on(zl, -d))
+        wait(b_z[t][d - 1], ref)
+        if d != 1:
+            same(ref, X_UP, OUT_C, b_one[t][0 if d == 2 else 1])
+        if d != 2:
+            same(ref, X_DN, OUT_C, b_one[t][2 if d == 1 else 3])
+
+    def last_x(t):
+        same(b_ref(t, x, on(zl, -1)), X_UP, OUT_C, b_up[t])
+        same(b_ref(t, x, on(zl, -2)), X_DN, OUT_C, b_dn[t])
 
     def forward(t, d):
         up_ref, dn_ref = b_ref(t, xm, on(zl, -d)), b_ref(t, xp, on(zl, -d))
@@ -347,17 +351,22 @@
             total = total + iz_recv[t, k].astype(F32)
         ig[t] = rounded(total)
 
-    for t in range(PARTS):
-        for d in (2, 1, 3):
-            from_z(t, d)
+    from_z(0, 2)
+    from_z(0, 1)
+    from_z(0, 3)
+    last_x(0)
+    forward(0, 2)
+    forward(0, 1)
+    from_z(1, 2)
+    from_z(1, 1)
+    from_z(1, 3)
+    forward(0, 3)
+    last_x(1)
 
     for where in L_TO:
         same(h(row), where, OUT_H, h_z)
     wait(s_wg, wg.at[sib])
     wait(s_wu, wu.at[sib])
-    forward(0, 2)
-    forward(0, 1)
-    forward(0, 3)
     forward(1, 2)
     wait(b_up[0], backs.at[0, pl.ds(0, 2)])
     wait(b_dn[0], backs.at[0, pl.ds(0, 2)])
@@ -366,10 +375,6 @@
     forward(1, 3)
     wait(b_far[0], backs.at[0, pl.ds(0, 4)])
     use(0, (xo,))
-    wait(h_z, hidden.at[:, :, pl.ds(0, 3)])
-    for d in (1, 2, 3):
-        for where in (X_OP, X_UP, X_DN):
-            same(h(at(x, on(zl, -d))), where, OUT_H, h_x)
     wait(i_y, inputs.at[0, :, pl.ds(0, 12)])
     s_i = arrival()
     same(inputs.at[core], SIB, OUT_H, s_i)
@@ -377,10 +382,19 @@
     wait(b_up[1], backs.at[1, pl.ds(0, 2)])
     wait(b_dn[1], backs.at[1, pl.ds(0, 2)])
     use(1, (x, xm, xp))
+
+    def hidden_x():
+        wait(h_z, hidden.at[:, :, pl.ds(0, 3)])
+        for d in (1, 2, 3):
+            for where in (X_OP, X_UP, X_DN):
+                same(h(at(x, on(zl, -d))), where, OUT_H, h_x)
+
+    pl.when(core == 0)(hidden_x)
     along_h(0)
     wait(b_far[1], backs.at[1, pl.ds(0, 4)])
     use(1, (xo,))
     along_h(1)
+    pl.when(core == 1)(hidden_x)
 
     def tokens(value):
         return value.reshape(512, value.shape[-1])

time: 84.1 us -> 80.6 us (0.958)
  the two profiles are of different devices: /device:TPU:24 before, /device:TPU:48 now
where the time goes in v4:
time: 80.6 us; the launch traced here: 80.5 us
  Pallas kernels  79.8 us (99%)
    pallas_call x1, Pallas kernels, shards(): pl.pallas_call(kernel, out_shape=shapes, in_specs=[any_space] * 7, out_sp...  77.6 us
    pallas_call x1, Pallas kernels, shards(): pl.pallas_call(hand_over, out_shape=shapes, in_specs=[any_space] * 4, out...  2.2 us

profile of v4, /device:TPU:48, one launch (start us, length us, event | category | flops | bytes accessed | tf_op | source)
XLA Modules:
  0.0 80.5 jit_solution(2820387926479683685)
XLA Ops:
  0.6 77.6 %swiglu_back.1 = (bf16[2,16,512]{2,1,0:T(8,128)(2,1)}, bf16[462,512]{1,0:T(8,128)(2,1)}, bf16[462,512]{1,0:T(8,128)(2,1)}, bf16[462,512]{1,0:T(8,128)(2,1)}) custom-call(bf16[2,16,512]{2,1,0:T(8,128)(2,1)} %bitcast.7, bf16[2,16,512]{2,1,0:T(8,128)(2,1)} %bitcast.8, bf16[64,462]{1,0:T(8,128)(2,1)} %gp_in.1, bf16[64,462]{1,0:T(8,128)(2,1)} %up_in.1, ...), custom_call_target="tpu_custom_call" | custom-call | flops 2906652672 | bytes 3000000 | tf_op jit(solution)/shard_map/swiglu_back/pallas_call | solution.py:456
  78.3 2.2 %hand_over.1 = (bf16[2,16,512]{2,1,0:T(8,128)(2,1)}, bf16[462,512]{1,0:T(8,128)(2,1)}, bf16[462,512]{1,0:T(8,128)(2,1)}, bf16[462,512]{1,0:T(8,128)(2,1)}) custom-call(bf16[2,16,512]{2,1,0:T(8,128)(2,1)} %get-tuple-element.12.refs_0_, bf16[462,512]{1,0:T(8,128)(2,1)} %get-tuple-element.13.refs_1_, bf16[462,512]{1,0:T(8,128)(2,1)} %get-tuple-element.14.refs_2_, ...), custom_call_target="tpu_custom_call" | custom-call | tf_op jit(solution)/shard_map/hand_over/pallas_call | solution.py:499

commit v5 on v4

--- a/solution.py
+++ b/solution.py
@@ -9,7 +9,7 @@
 F32 = jnp.float32
 MESH = pl.DeviceIdType.MESH
 N_GROUPS = 7
-N_ARRIVALS = 60
+N_ARRIVALS = 56
 WIDE = 512
 PARTS = 2
 RT = 32 // PARTS
@@ -34,7 +34,7 @@
     ig_out, dg_out, gg_out, ug_out,
     grads, inputs, hidden, backs, backs_sib,
     gp, up, pre, wd_raw, wg_raw, wu_raw, wd, wg, wu,
-    part, part_bf, far_lo, far_hi, from_lo, from_hi, z_send, z_recv,
+    part, part_bf, x_recv, z_send, z_recv,
     iq, iq_bf, i_recv, iz_send, iz_recv,
     gg, ug, dg, ig,
     local_sem, send_sem, recv_sem,
@@ -110,7 +110,7 @@
     c_li = local(li_in, inputs.at[core, :, own])
 
     barrier = pltpu.get_barrier_semaphore()
-    partners = [X_UP, X_DN, X_OP, Y_UP, Y_DN, Y_OP, H_UP, H_DN, H_OP, SIB] + L_TO
+    partners = [X_UP, X_DN, X_OP, Y_UP, Y_DN, Y_OP, H_UP, H_DN, SIB] + L_TO
     for where in partners:
         pl.semaphore_signal(barrier, inc=1, device_id=where, device_id_type=MESH)
     pl.semaphore_wait(barrier, len(partners))
@@ -125,9 +125,8 @@
     TO_Y = (Y_OP, Y_UP, Y_DN)
     g_z = [[arrival() for _ in range(3)] for _ in range(PARTS)]
     g_own = arrival()
-    for t in range(PARTS):
-        for k in range(3):
-            send(og_in.at[t], gt(t, own), TO_H[k][1], OUT_A, g_z[t][k])
+    for t, k in ((0, 1), (1, 2), (1, 1), (0, 2)):
+        send(og_in.at[t], gt(t, own), TO_H[k][1], OUT_A, g_z[t][k])
     for where in TO_Y:
         send(og_in, g(own), where, OUT_A, g_own)
 
@@ -157,16 +156,21 @@
         return hidden.at[:, :, block]
 
     h_x, h_z = arrival(), arrival()
+    h_one = [arrival() for _ in range(4)]
     for where in (X_OP, X_UP, X_DN):
         same(h(row), where, OUT_H, h_x)
 
     g_y = [arrival() for _ in range(PARTS)]
-    for t in range(PARTS):
-        for k in (1, 2, 0):
-            block = gt(t, at(y, TO_H[k][0]))
-            wait(g_z[t][k], block)
-            for where in TO_Y:
-                same(block, where, OUT_A, g_y[t])
+    def g_from_z(t, k):
+        block = gt(t, at(y, TO_H[k][0]))
+        wait(g_z[t][k], block)
+        if (t, k) in ((0, 1), (1, 2)):
+            same(block, TO_H[k][1], OUT_A, g_z[t][0])
+        for where in TO_Y:
+            same(block, where, OUT_A, g_y[t])
+
+    for t, k in ((0, 1), (1, 2), (0, 2), (1, 1), (0, 0), (1, 0)):
+        g_from_z(t, k)
 
     def li(block):
         return inputs.at[core, :, block]
@@ -181,36 +185,22 @@
         part[t * 2 + j] = out
         part_bf[t * 2 + j] = rounded(out)
 
-    def two(ref, u, a, b):
-        return ref.at[u, pl.ds(a * 4 + b, 2)]
-
     n_units = 2 * PARTS
-    r_up = [arrival() for _ in range(n_units)]
-    r_dn = [arrival() for _ in range(n_units)]
     x_in = [arrival() for _ in range(n_units)]
     z_in = [arrival() for _ in range(n_units)]
 
     def begin(u):
-        send(two(part_bf, u, xo, 0), far_lo.at[u], X_UP, OUT_B, r_up[u])
-        send(two(part_bf, u, xo, 2), far_hi.at[u], X_DN, OUT_B, r_dn[u])
-        send(two(part_bf, u, xp, 2), from_lo.at[u, pl.ds(2, 2)], X_UP, OUT_B, x_in[u])
-        send(two(part_bf, u, xm, 0), from_hi.at[u, pl.ds(0, 2)], X_DN, OUT_B, x_in[u])
-
-    def late(u):
-        wait(r_up[u], far_lo.at[u])
-        lo = pl.ds(xp * 4, 2)
-        part_bf[u, lo] = rounded(part[u, lo] + far_lo[u].astype(F32))
-        send(two(part_bf, u, xp, 0), from_lo.at[u, pl.ds(0, 2)], X_UP, OUT_B, x_in[u])
-        wait(r_dn[u], far_hi.at[u])
-        hi = pl.ds(xm * 4 + 2, 2)
-        part_bf[u, hi] = rounded(part[u, hi] + far_hi[u].astype(F32))
-        send(two(part_bf, u, xm, 2), from_hi.at[u, pl.ds(2, 2)], X_DN, OUT_B, x_in[u])
+        for k, (a, where) in enumerate(((xo, X_OP), (xp, X_UP), (xm, X_DN))):
+            send(part_bf.at[u, pl.ds(a * 4, 4)], x_recv.at[u, k], where, OUT_B, x_in[u])
 
     def x_sum(u, b):
-        return part[u, at(x, b)] + from_lo[u, b].astype(F32) + from_hi[u, b].astype(F32)
+        out = part[u, at(x, b)]
+        for k in range(3):
+            out = out + x_recv[u, k, b].astype(F32)
+        return out
 
     def along_z(u):
-        wait(x_in[u], part_bf.at[u, pl.ds(0, 8)])
+        wait(x_in[u], x_recv.at[u])
         for d in (2, 1, 3):
             z_send[u, d - 1] = rounded(x_sum(u, on(zl, d)))
             send(z_send.at[u, d - 1], z_recv.at[u, d - 1], L_TO[d - 1], OUT_B, z_in[u])
@@ -223,17 +213,13 @@
     begin(0)
     partial(0, 1)
     begin(1)
-    late(0)
     wait(g_y[1], grads.at[0, 0, pl.ds(0, 9)])
     partial(1, 0)
     begin(2)
-    late(1)
     partial(1, 1)
     begin(3)
     along_z(0)
-    late(2)
     along_z(1)
-    late(3)
     s_g = arrival()
     same(grads.at[core], SIB, OUT_W, s_g)
     s_wg = padded(wg_raw, wg, c_wg)
@@ -385,22 +371,39 @@
 
     def hidden_x():
         wait(h_z, hidden.at[:, :, pl.ds(0, 3)])
-        for d in (1, 2, 3):
-            for where in (X_OP, X_UP, X_DN):
-                same(h(at(x, on(zl, -d))), where, OUT_H, h_x)
-
+        one, two, three = [h(at(x, on(zl, -d))) for d in (1, 2, 3)]
+        same(two, X_UP, OUT_H, h_one[0])
+        same(one, X_DN, OUT_H, h_one[2])
+        same(three, X_UP, OUT_H, h_one[1])
+        same(three, X_DN, OUT_H, h_one[3])
+        same(one, X_UP, OUT_H, h_x)
+        same(two, X_DN, OUT_H, h_x)
+
+    def hidden_forward():
+        ref = h(at(xm, on(zl, -2)))
+        wait(h_one[0], ref)
+        same(ref, X_UP, OUT_H, h_x)
+        ref = h(at(xp, on(zl, -1)))
+        wait(h_one[2], ref)
+        same(ref, X_DN, OUT_H, h_x)
+        wait(h_one[1], ref)
+        same(hidden.at[0, :, at(xm, on(zl, -3))], X_UP, OUT_H, h_x)
+        wait(h_one[3], ref)
+        same(hidden.at[1, :, at(xp, on(zl, -3))], X_DN, OUT_H, h_x)
+
+    wait(b_far[1], backs.at[1, pl.ds(0, 4)])
     pl.when(core == 0)(hidden_x)
+    use(1, (xo,))
     along_h(0)
-    wait(b_far[1], backs.at[1, pl.ds(0, 4)])
-    use(1, (xo,))
     along_h(1)
-    pl.when(core == 1)(hidden_x)
 
     def tokens(value):
         return value.reshape(512, value.shape[-1])
 
     wait(s_i, inputs.at[sib])
+    pl.when(core == 1)(hidden_x)
     wait(s_b, backs_sib)
+    hidden_forward()
     outs = []
     for k, ref, out in ((0, gg, gg_out), (1, ug, ug_out)):
         value = dot(tokens(backs[:, :, k, core]), tokens(inputs[core]), TN)
@@ -408,7 +411,7 @@
         ref[...] = rounded(value[0:units, :])
         outs.append(local(ref, out))
     finish(0)
-    wait(h_x, hidden.at[:, :, pl.ds(0, 12)])
+    wait(h_x, hidden.at[0])
     wait(s_g, grads.at[sib])
     dg[...] = rounded(
         dot(hidden[...].reshape(1024, WIDE), grads[...].reshape(1024, feats), TN)[0:units, :]
@@ -468,8 +471,7 @@
             vm((units, feats), BF), vm((units, feats), BF), vm((units, feats), BF),
             vm((2, WIDE, feats), BF), vm((2, WIDE, feats), BF), vm((2, WIDE, feats), BF),
             vm((2 * PARTS, 16, RT, WIDE), F32), vm((2 * PARTS, 16, RT, WIDE), BF),
-            vm((2 * PARTS, 2, RT, WIDE), BF), vm((2 * PARTS, 2, RT, WIDE), BF),
-            vm((2 * PARTS, 4, RT, WIDE), BF), vm((2 * PARTS, 4, RT, WIDE), BF),
+            vm((2 * PARTS, 3, 4, RT, WIDE), BF),
             vm((2 * PARTS, 3, RT, WIDE), BF), vm((2 * PARTS, 3, RT, WIDE), BF),
             vm((PARTS, 16, RT, feats), F32), vm((PARTS, 16, RT, feats), BF),
             vm((PARTS, 4, 4, RT, feats), BF),

time: 80.6 us -> 77.5 us (0.962)
  Pallas kernels: 79.8 us -> 76.7 us
    pallas_call x1, Pallas kernels: 77.6 us -> 74.5 us  [shards(): pl.pallas_call(kernel, out_shape=shapes, in_specs=[any_space] * 7, out_sp...]
where the time goes in v5:
time: 77.5 us; the launch traced here: 77.4 us
  Pallas kernels  76.7 us (99%)
    pallas_call x1, Pallas kernels, shards(): pl.pallas_call(kernel, out_shape=shapes, in_specs=[any_space] * 7, out_sp...  74.5 us
    pallas_call x1, Pallas kernels, shards(): pl.pallas_call(hand_over, out_shape=shapes, in_specs=[any_space] * 4, out...  2.2 us

profile of v5, /device:TPU:48, one launch (start us, length us, event | category | flops | bytes accessed | tf_op | source)
XLA Modules:
  0.0 77.4 jit_solution(4238423245557330429)
XLA Ops:
  0.6 74.5 %swiglu_back.1 = (bf16[2,16,512]{2,1,0:T(8,128)(2,1)}, bf16[462,512]{1,0:T(8,128)(2,1)}, bf16[462,512]{1,0:T(8,128)(2,1)}, bf16[462,512]{1,0:T(8,128)(2,1)}) custom-call(bf16[2,16,512]{2,1,0:T(8,128)(2,1)} %bitcast.7, bf16[2,16,512]{2,1,0:T(8,128)(2,1)} %bitcast.8, bf16[64,462]{1,0:T(8,128)(2,1)} %gp_in.1, bf16[64,462]{1,0:T(8,128)(2,1)} %up_in.1, ...), custom_call_target="tpu_custom_call" | custom-call | flops 2906652672 | bytes 3000000 | tf_op jit(solution)/shard_map/swiglu_back/pallas_call | solution.py:459
  75.2 2.2 %hand_over.1 = (bf16[2,16,512]{2,1,0:T(8,128)(2,1)}, bf16[462,512]{1,0:T(8,128)(2,1)}, bf16[462,512]{1,0:T(8,128)(2,1)}, bf16[462,512]{1,0:T(8,128)(2,1)}) custom-call(bf16[2,16,512]{2,1,0:T(8,128)(2,1)} %get-tuple-element.12.refs_0_, bf16[462,512]{1,0:T(8,128)(2,1)} %get-tuple-element.13.refs_1_, bf16[462,512]{1,0:T(8,128)(2,1)} %get-tuple-element.14.refs_2_, ...), custom_call_target="tpu_custom_call" | custom-call | tf_op jit(solution)/shard_map/hand_over/pallas_call | solution.py:501

commit v6 on v5

--- a/solution.py
+++ b/solution.py
@@ -9,7 +9,7 @@
 F32 = jnp.float32
 MESH = pl.DeviceIdType.MESH
 N_GROUPS = 7
-N_ARRIVALS = 56
+N_ARRIVALS = 58
 WIDE = 512
 PARTS = 2
 RT = 32 // PARTS
@@ -125,7 +125,7 @@
     TO_Y = (Y_OP, Y_UP, Y_DN)
     g_z = [[arrival() for _ in range(3)] for _ in range(PARTS)]
     g_own = arrival()
-    for t, k in ((0, 1), (1, 2), (1, 1), (0, 2)):
+    for t, k in ((0, 1), (1, 2)):
         send(og_in.at[t], gt(t, own), TO_H[k][1], OUT_A, g_z[t][k])
     for where in TO_Y:
         send(og_in, g(own), where, OUT_A, g_own)
@@ -166,6 +166,7 @@
         wait(g_z[t][k], block)
         if (t, k) in ((0, 1), (1, 2)):
             same(block, TO_H[k][1], OUT_A, g_z[t][0])
+            send(og_in.at[1 - t], gt(1 - t, own), TO_H[k][1], OUT_A, g_z[1 - t][k])
         for where in TO_Y:
             same(block, where, OUT_A, g_y[t])
 
@@ -178,6 +179,39 @@
     i_z = arrival()
     for _, where in TO_H:
         send(li_in, li(own), where, OUT_A, i_z)
+
+    def on_core(k, what, *args):
+        @pl.when(core == k)
+        def _():
+            what(*args)
+
+    def hidden_z():
+        for where in L_TO:
+            same(h(row), where, OUT_H, h_z)
+
+    def hidden_x():
+        wait(h_z, hidden.at[:, :, pl.ds(0, 3)])
+        one, two, three = [h(at(x, on(zl, -d))) for d in (1, 2, 3)]
+        same(two, X_UP, OUT_H, h_one[0])
+        same(one, X_DN, OUT_H, h_one[2])
+        same(three, X_UP, OUT_H, h_one[1])
+        same(three, X_DN, OUT_H, h_one[3])
+        same(one, X_UP, OUT_H, h_x)
+        same(two, X_DN, OUT_H, h_x)
+
+    def hidden_forward():
+        ref = h(at(xm, on(zl, -2)))
+        wait(h_one[0], ref)
+        same(ref, X_UP, OUT_H, h_x)
+        ref = h(at(xp, on(zl, -1)))
+        wait(h_one[2], ref)
+        same(ref, X_DN, OUT_H, h_x)
+        wait(h_one[1], ref)
+        same(hidden.at[0, :, at(xm, on(zl, -3))], X_UP, OUT_H, h_x)
+        wait(h_one[3], ref)
+        same(hidden.at[1, :, at(xp, on(zl, -3))], X_DN, OUT_H, h_x)
+
+    on_core(1, hidden_z)
 
     def partial(t, j):
         rows = grads[core, t].reshape(16 * RT, feats)
@@ -227,6 +261,7 @@
     along_z(2)
 
     along_z(3)
+    on_core(1, hidden_x)
     wait(s_pre, pre.at[sib, core])
 
     def b_ref(t, a, b):
@@ -237,6 +272,7 @@
     b_up = [arrival() for _ in range(PARTS)]
     b_dn = [arrival() for _ in range(PARTS)]
     b_far = [arrival() for _ in range(PARTS)]
+    b_opp = [arrival() for _ in range(PARTS)]
 
     def start_backs(t):
         for j in (0, 1):
@@ -253,7 +289,8 @@
             backs[t, row, 1, j] = rounded(back * gate * sig)
         for d in (2, 1, 3):
             same(backs.at[t, row], L_TO[d - 1], OUT_C, b_z[t][d - 1])
-        same(backs.at[t, row], X_OP, OUT_C, b_far[t])
+        on_core(0, same, backs.at[t, row], X_OP, OUT_C, b_opp[t])
+        on_core(1, same, backs.at[t, row], X_OP, OUT_C, b_far[t])
         same(backs.at[t, row], X_UP, OUT_C, b_up[t])
         same(backs.at[t, row], X_DN, OUT_C, b_dn[t])
 
@@ -273,6 +310,18 @@
             same(ref, X_UP, OUT_C, b_one[t][0 if d == 2 else 1])
         if d != 2:
             same(ref, X_DN, OUT_C, b_one[t][2 if d == 1 else 3])
+
+    def opposite_to_z(t):
+        ref = b_ref(t, xo, zl)
+        wait(b_opp[t], ref)
+        for d in (2, 1, 3):
+            same(ref, L_TO[d - 1], OUT_C, b_far[t])
+
+    def from_z_last(t, d):
+        ref = b_ref(t, x, on(zl, -d))
+        wait(b_z[t][d - 1], ref)
+        same(ref, X_UP, OUT_C, b_up[t])
+        same(ref, X_DN, OUT_C, b_dn[t])
 
     def last_x(t):
         same(b_ref(t, x, on(zl, -1)), X_UP, OUT_C, b_up[t])
@@ -337,73 +386,65 @@
             total = total + iz_recv[t, k].astype(F32)
         ig[t] = rounded(total)
 
-    from_z(0, 2)
-    from_z(0, 1)
-    from_z(0, 3)
-    last_x(0)
-    forward(0, 2)
-    forward(0, 1)
-    from_z(1, 2)
-    from_z(1, 1)
-    from_z(1, 3)
-    forward(0, 3)
-    last_x(1)
-
-    for where in L_TO:
-        same(h(row), where, OUT_H, h_z)
+    def gather_0():
+        for t in range(PARTS):
+            opposite_to_z(t)
+            for d in (2, 1, 3):
+                from_z_last(t, d)
+        hidden_z()
+
+    def gather_1():
+        for d in (2, 1, 3):
+            from_z(0, d)
+        last_x(0)
+        hidden_forward()
+        forward(0, 2)
+        forward(0, 1)
+        for d in (2, 1, 3):
+            from_z(1, d)
+        forward(0, 3)
+        last_x(1)
+        forward(1, 2)
+
+    on_core(0, gather_0)
+    on_core(1, gather_1)
+
+    def near_planes(t):
+        for k, blocks in ((0, 4), (1, 2)):
+            on_core(k, wait, b_up[t], backs.at[t, pl.ds(0, blocks)])
+            on_core(k, wait, b_dn[t], backs.at[t, pl.ds(0, blocks)])
+
+    def far_plane(t):
+        for k, blocks in ((0, 3), (1, 4)):
+            on_core(k, wait, b_far[t], backs.at[t, pl.ds(0, blocks)])
+
     wait(s_wg, wg.at[sib])
     wait(s_wu, wu.at[sib])
-    forward(1, 2)
-    wait(b_up[0], backs.at[0, pl.ds(0, 2)])
-    wait(b_dn[0], backs.at[0, pl.ds(0, 2)])
+    near_planes(0)
     use(0, (x, xm, xp))
-    forward(1, 1)
-    forward(1, 3)
-    wait(b_far[0], backs.at[0, pl.ds(0, 4)])
+    on_core(1, forward, 1, 1)
+    on_core(1, forward, 1, 3)
+    far_plane(0)
     use(0, (xo,))
     wait(i_y, inputs.at[0, :, pl.ds(0, 12)])
     s_i = arrival()
     same(inputs.at[core], SIB, OUT_H, s_i)
 
-    wait(b_up[1], backs.at[1, pl.ds(0, 2)])
-    wait(b_dn[1], backs.at[1, pl.ds(0, 2)])
+    near_planes(1)
     use(1, (x, xm, xp))
 
-    def hidden_x():
-        wait(h_z, hidden.at[:, :, pl.ds(0, 3)])
-        one, two, three = [h(at(x, on(zl, -d))) for d in (1, 2, 3)]
-        same(two, X_UP, OUT_H, h_one[0])
-        same(one, X_DN, OUT_H, h_one[2])
-        same(three, X_UP, OUT_H, h_one[1])
-        same(three, X_DN, OUT_H, h_one[3])
-        same(one, X_UP, OUT_H, h_x)
-        same(two, X_DN, OUT_H, h_x)
-
-    def hidden_forward():
-        ref = h(at(xm, on(zl, -2)))
-        wait(h_one[0], ref)
-        same(ref, X_UP, OUT_H, h_x)
-        ref = h(at(xp, on(zl, -1)))
-        wait(h_one[2], ref)
-        same(ref, X_DN, OUT_H, h_x)
-        wait(h_one[1], ref)
-        same(hidden.at[0, :, at(xm, on(zl, -3))], X_UP, OUT_H, h_x)
-        wait(h_one[3], ref)
-        same(hidden.at[1, :, at(xp, on(zl, -3))], X_DN, OUT_H, h_x)
-
-    wait(b_far[1], backs.at[1, pl.ds(0, 4)])
-    pl.when(core == 0)(hidden_x)
+    far_plane(1)
     use(1, (xo,))
     along_h(0)
+    on_core(0, hidden_x)
     along_h(1)
 
     def tokens(value):
         return value.reshape(512, value.shape[-1])
 
     wait(s_i, inputs.at[sib])
-    pl.when(core == 1)(hidden_x)
     wait(s_b, backs_sib)
-    hidden_forward()
+    on_core(0, hidden_forward)
     outs = []
     for k, ref, out in ((0, gg, gg_out), (1, ug, ug_out)):
         value = dot(tokens(backs[:, :, k, core]), tokens(inputs[core]), TN)

time: 77.5 us -> 75.1 us (0.969)
  the two profiles are of different devices: /device:TPU:48 before, /device:TPU:24 now
where the time goes in v6:
time: 75.1 us; the launch traced here: 73.9 us
  Pallas kernels  73.3 us (98%)
    pallas_call x1, Pallas kernels, shards(): pl.pallas_call(kernel, out_shape=shapes, in_specs=[any_space] * 7, out_sp...  71.1 us
    pallas_call x1, Pallas kernels, shards(): pl.pallas_call(hand_over, out_shape=shapes, in_specs=[any_space] * 4, out...  2.2 us

profile of v6, /device:TPU:24, one launch (start us, length us, event | category | flops | bytes accessed | tf_op | source)
XLA Modules:
  0.0 73.9 jit_solution(3807927109537542192)
XLA Ops:
  0.6 71.1 %swiglu_back.1 = (bf16[2,16,512]{2,1,0:T(8,128)(2,1)}, bf16[462,512]{1,0:T(8,128)(2,1)}, bf16[462,512]{1,0:T(8,128)(2,1)}, bf16[462,512]{1,0:T(8,128)(2,1)}) custom-call(bf16[2,16,512]{2,1,0:T(8,128)(2,1)} %bitcast.7, bf16[2,16,512]{2,1,0:T(8,128)(2,1)} %bitcast.8, bf16[64,462]{1,0:T(8,128)(2,1)} %gp_in.1, bf16[64,462]{1,0:T(8,128)(2,1)} %up_in.1, ...), custom_call_target="tpu_custom_call" | custom-call | flops 2906652672 | bytes 3000000 | tf_op jit(solution)/shard_map/swiglu_back/pallas_call | solution.py:500
  71.7 2.2 %hand_over.1 = (bf16[2,16,512]{2,1,0:T(8,128)(2,1)}, bf16[462,512]{1,0:T(8,128)(2,1)}, bf16[462,512]{1,0:T(8,128)(2,1)}, bf16[462,512]{1,0:T(8,128)(2,1)}) custom-call(bf16[2,16,512]{2,1,0:T(8,128)(2,1)} %get-tuple-element.12.refs_0_, bf16[462,512]{1,0:T(8,128)(2,1)} %get-tuple-element.13.refs_1_, bf16[462,512]{1,0:T(8,128)(2,1)} %get-tuple-element.14.refs_2_, ...), custom_call_target="tpu_custom_call" | custom-call | tf_op jit(solution)/shard_map/hand_over/pallas_call | solution.py:542

commit v7 on v6

--- a/solution.py
+++ b/solution.py
@@ -274,6 +274,13 @@
     b_far = [arrival() for _ in range(PARTS)]
     b_opp = [arrival() for _ in range(PARTS)]
 
+    def over_three(d):
+        return zl == {1: 3, 2: 4, 3: 0}[d]
+
+    def pass_on(t, ref):
+        pl.when(zl == 2)(lambda: same(ref, L_TO[0], OUT_C, b_z[t][2]))
+        pl.when(zl == 1)(lambda: same(ref, L_TO[2], OUT_C, b_z[t][0]))
+
     def start_backs(t):
         for j in (0, 1):
             u = t * 2 + j
@@ -288,7 +295,9 @@
             backs[t, row, 0, j] = rounded(back * upper * sig * (1.0 + gate * (1.0 - sig)))
             backs[t, row, 1, j] = rounded(back * gate * sig)
         for d in (2, 1, 3):
-            same(backs.at[t, row], L_TO[d - 1], OUT_C, b_z[t][d - 1])
+            pl.when(jnp.logical_not(over_three(d)))(
+                lambda d=d: same(backs.at[t, row], L_TO[d - 1], OUT_C, b_z[t][d - 1])
+            )
         on_core(0, same, backs.at[t, row], X_OP, OUT_C, b_opp[t])
         on_core(1, same, backs.at[t, row], X_OP, OUT_C, b_far[t])
         same(backs.at[t, row], X_UP, OUT_C, b_up[t])
@@ -306,6 +315,8 @@
     def from_z(t, d):
         ref = b_ref(t, x, on(zl, -d))
         wait(b_z[t][d - 1], ref)
+        if d == 2:
+            pass_on(t, ref)
         if d != 1:
             same(ref, X_UP, OUT_C, b_one[t][0 if d == 2 else 1])
         if d != 2:
@@ -320,6 +331,8 @@
     def from_z_last(t, d):
         ref = b_ref(t, x, on(zl, -d))
         wait(b_z[t][d - 1], ref)
+        if d == 2:
+            pass_on(t, ref)
         same(ref, X_UP, OUT_C, b_up[t])
         same(ref, X_DN, OUT_C, b_dn[t])
 
@@ -409,32 +422,37 @@
     on_core(0, gather_0)
     on_core(1, gather_1)
 
-    def near_planes(t):
-        for k, blocks in ((0, 4), (1, 2)):
-            on_core(k, wait, b_up[t], backs.at[t, pl.ds(0, blocks)])
-            on_core(k, wait, b_dn[t], backs.at[t, pl.ds(0, blocks)])
-
     def far_plane(t):
         for k, blocks in ((0, 3), (1, 4)):
             on_core(k, wait, b_far[t], backs.at[t, pl.ds(0, blocks)])
 
     wait(s_wg, wg.at[sib])
     wait(s_wu, wu.at[sib])
-    near_planes(0)
-    use(0, (x, xm, xp))
-    on_core(1, forward, 1, 1)
-    on_core(1, forward, 1, 3)
-    far_plane(0)
-    use(0, (xo,))
+    def chunk_0(t):
+        far_plane(t)
+        use(t, (x, xo))
+        wait(b_up[t], backs.at[t, pl.ds(0, 4)])
+        use(t, (xm,))
+        wait(b_dn[t], backs.at[t, pl.ds(0, 4)])
+        use(t, (xp,))
+
+    def chunk_1(t):
+        wait(b_up[t], backs.at[t, pl.ds(0, 2)])
+        wait(b_dn[t], backs.at[t, pl.ds(0, 2)])
+        use(t, (x, xm, xp))
+        if t == 0:
+            forward(1, 1)
+            forward(1, 3)
+        far_plane(t)
+        use(t, (xo,))
+
+    on_core(0, chunk_0, 0)
+    on_core(1, chunk_1, 0)
     wait(i_y, inputs.at[0, :, pl.ds(0, 12)])
     s_i = arrival()
     same(inputs.at[core], SIB, OUT_H, s_i)
-
-    near_planes(1)
-    use(1, (x, xm, xp))
-
-    far_plane(1)
-    use(1, (xo,))
+    on_core(0, chunk_0, 1)
+    on_core(1, chunk_1, 1)
     along_h(0)
     on_core(0, hidden_x)
     along_h(1)
@@ -465,7 +483,9 @@
     wait_sent(OUT_W, backs)
     wait_sent(OUT_H, backs.at[:, pl.ds(0, 15)])
     wait_sent(OUT_B, grads.at[:, :, pl.ds(0, 15)])
-    wait_sent(OUT_C, backs.at[:, pl.ds(0, 15)])
+    ends = jnp.logical_or(zl == 0, zl == 3)
+    pl.when(ends)(lambda: wait_sent(OUT_C, backs.at[:, pl.ds(0, 14)]))
+    pl.when(jnp.logical_not(ends))(lambda: wait_sent(OUT_C, backs))
     wait_sent(OUT_S, backs.at[0])
     wait_sent(OUT_D, grads.at[0, :, pl.ds(0, 15)])
     for copy in outs:

time: 75.1 us -> 75 us (level); the launches traced: 73.9 us -> 74.9 us
  Pallas kernels: 73.3 us -> 74.2 us
    pallas_call x1, Pallas kernels: 71.1 us -> 72 us  [shards(): pl.pallas_call(kernel, out_shape=shapes, in_specs=[any_space] * 7, out_sp...]
where the time goes in v7:
time: 75 us; the launch traced here: 74.9 us
  Pallas kernels  74.2 us (99%)
    pallas_call x1, Pallas kernels, shards(): pl.pallas_call(kernel, out_shape=shapes, in_specs=[any_space] * 7, out_sp...  72 us
    pallas_call x1, Pallas kernels, shards(): pl.pallas_call(hand_over, out_shape=shapes, in_specs=[any_space] * 4, out...  2.2 us

profile of v7, /device:TPU:24, one launch (start us, length us, event | category | flops | bytes accessed | tf_op | source)
XLA Modules:
  0.0 74.9 jit_solution(8856170214856030811)
XLA Ops:
  0.6 72.0 %swiglu_back.1 = (bf16[2,16,512]{2,1,0:T(8,128)(2,1)}, bf16[462,512]{1,0:T(8,128)(2,1)}, bf16[462,512]{1,0:T(8,128)(2,1)}, bf16[462,512]{1,0:T(8,128)(2,1)}) custom-call(bf16[2,16,512]{2,1,0:T(8,128)(2,1)} %bitcast.7, bf16[2,16,512]{2,1,0:T(8,128)(2,1)} %bitcast.8, bf16[64,462]{1,0:T(8,128)(2,1)} %gp_in.1, bf16[64,462]{1,0:T(8,128)(2,1)} %up_in.1, ...), custom_call_target="tpu_custom_call" | custom-call | flops 2906652672 | bytes 3000000 | tf_op jit(solution)/shard_map/swiglu_back/pallas_call | solution.py:520
  72.7 2.2 %hand_over.1 = (bf16[2,16,512]{2,1,0:T(8,128)(2,1)}, bf16[462,512]{1,0:T(8,128)(2,1)}, bf16[462,512]{1,0:T(8,128)(2,1)}, bf16[462,512]{1,0:T(8,128)(2,1)}) custom-call(bf16[2,16,512]{2,1,0:T(8,128)(2,1)} %get-tuple-element.12.refs_0_, bf16[462,512]{1,0:T(8,128)(2,1)} %get-tuple-element.13.refs_1_, bf16[462,512]{1,0:T(8,128)(2,1)} %get-tuple-element.14.refs_2_, ...), custom_call_target="tpu_custom_call" | custom-call | tf_op jit(solution)/shard_map/hand_over/pallas_call | solution.py:562

commit v8 on v7

--- a/solution.py
+++ b/solution.py
@@ -62,6 +62,11 @@
     L_TO = [(at(x, on(zl, d)), col) for d in (1, 2, 3)]
     SIB = (row, at(y, zh) * 2 + sib)
 
+    barrier = pltpu.get_barrier_semaphore()
+    partners = [H_UP, H_DN] + L_TO + [X_OP, Y_OP, X_UP, X_DN, Y_UP, Y_DN, SIB]
+    for where in partners:
+        pl.semaphore_signal(barrier, inc=1, device_id=where, device_id_type=MESH)
+
     locals_ = []
 
     def local(src, dst):
@@ -109,10 +114,6 @@
     c_wu = local(wu_in, wu_raw)
     c_li = local(li_in, inputs.at[core, :, own])
 
-    barrier = pltpu.get_barrier_semaphore()
-    partners = [X_UP, X_DN, X_OP, Y_UP, Y_DN, Y_OP, H_UP, H_DN, SIB] + L_TO
-    for where in partners:
-        pl.semaphore_signal(barrier, inc=1, device_id=where, device_id_type=MESH)
     pl.semaphore_wait(barrier, len(partners))
 
     def g(block):
@@ -418,6 +419,8 @@
         forward(0, 3)
         last_x(1)
         forward(1, 2)
+        forward(1, 1)
+        forward(1, 3)
 
     on_core(0, gather_0)
     on_core(1, gather_1)
@@ -440,9 +443,6 @@
         wait(b_up[t], backs.at[t, pl.ds(0, 2)])
         wait(b_dn[t], backs.at[t, pl.ds(0, 2)])
         use(t, (x, xm, xp))
-        if t == 0:
-            forward(1, 1)
-            forward(1, 3)
         far_plane(t)
         use(t, (xo,))
 

time: 75 us -> 75.8 us (1.011); the launches traced: 74.9 us -> 74.7 us
  no operation moved by 1% of the time
where the time goes in v8:
time: 75.8 us; the launch traced here: 74.7 us
  Pallas kernels  74.1 us (98%)
    pallas_call x1, Pallas kernels, shards(): pl.pallas_call(kernel, out_shape=shapes, in_specs=[any_space] * 7, out_sp...  71.9 us
    pallas_call x1, Pallas kernels, shards(): pl.pallas_call(hand_over, out_shape=shapes, in_specs=[any_space] * 4, out...  2.2 us

profile of v8, /device:TPU:24, one launch (start us, length us, event | category | flops | bytes accessed | tf_op | source)
XLA Modules:
  0.0 74.7 jit_solution(10993767635369956711)
XLA Ops:
  0.6 71.9 %swiglu_back.1 = (bf16[2,16,512]{2,1,0:T(8,128)(2,1)}, bf16[462,512]{1,0:T(8,128)(2,1)}, bf16[462,512]{1,0:T(8,128)(2,1)}, bf16[462,512]{1,0:T(8,128)(2,1)}) custom-call(bf16[2,16,512]{2,1,0:T(8,128)(2,1)} %bitcast.7, bf16[2,16,512]{2,1,0:T(8,128)(2,1)} %bitcast.8, bf16[64,462]{1,0:T(8,128)(2,1)} %gp_in.1, bf16[64,462]{1,0:T(8,128)(2,1)} %up_in.1, ...), custom_call_target="tpu_custom_call" | custom-call | flops 2906652672 | bytes 3000000 | tf_op jit(solution)/shard_map/swiglu_back/pallas_call | solution.py:520
  72.5 2.2 %hand_over.1 = (bf16[2,16,512]{2,1,0:T(8,128)(2,1)}, bf16[462,512]{1,0:T(8,128)(2,1)}, bf16[462,512]{1,0:T(8,128)(2,1)}, bf16[462,512]{1,0:T(8,128)(2,1)}) custom-call(bf16[2,16,512]{2,1,0:T(8,128)(2,1)} %get-tuple-element.12.refs_0_, bf16[462,512]{1,0:T(8,128)(2,1)} %get-tuple-element.13.refs_1_, bf16[462,512]{1,0:T(8,128)(2,1)} %get-tuple-element.14.refs_2_, ...), custom_call_target="tpu_custom_call" | custom-call | tf_op jit(solution)/shard_map/hand_over/pallas_call | solution.py:562
